TPU v7x, 512 devices: a whole 4x4x16 slice. The times are simulated.
512 devices in a mesh: head: 2 (over y_hi), inner: 16 (over x, y_lo, core), outer: 16 (over z).
Axes of the slice: x: 4, y: 4 (y_hi: 2, y_lo: 2; y = y_hi * 2 + y_lo), z: 16, core: 2. Of those that a mesh axis runs over, the one named last changes fastest.
Arguments:
- query: bfloat16 [16, 16, 256, 4096], P('outer', 'inner', 'head'), may hold values from -300 to 300
- dout: bfloat16 [16, 16, 256, 4096], P('outer', 'inner', 'head'), may hold values from -6 to 6
- key_mant: bfloat16 [16, 16, 256, 512], P('outer', 'inner', None, 'head'), may hold values from -6 to 6
- value_mantissas: bfloat16 [16, 16, 256, 512], P('outer', 'inner', None, 'head'), may hold values from -6 to 6
- key_exps: int32 [16, 16, 2, 4], P('outer', 'inner', None, 'head'), may hold values from -1 to 1
- value_exponents: int32 [16, 16, 2, 4], P('outer', 'inner', None, 'head'), may hold values from -1 to 1
- reach: int32 [16, 16], P('outer', 'inner'), may hold values from 64 to 256
Outputs:
- query_grad: bfloat16 [16, 16, 256, 4096], P('outer', 'inner', 'head')
- key_grad: bfloat16 [16, 16, 256, 512], P('outer', 'inner', None, 'head')
- value_grad: bfloat16 [16, 16, 256, 512], P('outer', 'inner', None, 'head')
All inputs are finite; a program needn't handle non-finite values.
Results may differ from a plain program's by a relative error of at most 0.013.
Values may be sent and summed in bfloat16 or wider, within the bound.
No kernel may reach another device: no remote copies, remote signals or barrier semaphores. Data moves between devices by JAX's collectives and lax.ppermute only.
A program may use at most 64 MiB of HBM per device.

v0:
```python
import jax
import jax.numpy as jnp
from jax import lax
from jax.sharding import PartitionSpec as P

QUERY_HEADS = 32
KEY_VALUE_HEADS = 4
HEAD_SIZE = 128


NEG_FILL = -1e30


def passed_along(value, axis, steps):
    count = lax.axis_size(axis)
    initial, last = (max(0, -steps), min(count, count - steps))
    return lax.ppermute(value, axis, [(source, source + steps) for source in range(initial, last)])


def expand(mantissa_values, scale_factors):
    blocks, head_count = scale_factors.shape
    length, row_width = mantissa_values.shape
    reshaped_array = mantissa_values.reshape(
        blocks, length // blocks, head_count, row_width // head_count
    )
    return (reshaped_array * scale_factors[:, None, :, None]).reshape(
        length, head_count, row_width // head_count
    )


def attend(
    queries, grads_out, own_keys, own_values, prev_keys, prev_values, first_cycle, reach_rows
):
    query_matrix = queries.shape[0]
    length = own_keys.shape[0]
    factor = HEAD_SIZE ** (-0.5)
    positions = jnp.arange(query_matrix)
    columns = jnp.arange(length)
    own_mask = columns[None, :] <= positions[:, None]
    prev_mask = jnp.logical_and(columns >= length - reach_rows, jnp.logical_not(first_cycle))

    def per_head(members):
        query_head, grad_head, key_own, value_own, key_prev, value_prev = members
        score_own = (
            jnp.einsum("tgd,sd->gts", query_head, key_own, preferred_element_type=jnp.float32)
            * factor
        )
        score_prev = (
            jnp.einsum("tgd,sd->gts", query_head, key_prev, preferred_element_type=jnp.float32)
            * factor
        )
        score_own = jnp.where(own_mask[None], score_own, NEG_FILL)
        score_prev = jnp.where(prev_mask[None, None], score_prev, NEG_FILL)
        row_peak = jnp.maximum(jnp.max(score_own, axis=2), jnp.max(score_prev, axis=2))
        weight_own = jnp.exp(score_own - row_peak[:, :, None])
        weight_prev = jnp.exp(score_prev - row_peak[:, :, None])
        weight_sum = jnp.sum(weight_own, axis=2) + jnp.sum(weight_prev, axis=2)
        weight_own = weight_own / weight_sum[:, :, None]
        weight_prev = weight_prev / weight_sum[:, :, None]
        rounded_own = weight_own.astype(jnp.bfloat16)
        rounded_prev = weight_prev.astype(jnp.bfloat16)
        output = jnp.einsum(
            "gts,sd->gtd", rounded_own, value_own, preferred_element_type=jnp.float32
        ) + jnp.einsum("gts,sd->gtd", rounded_prev, value_prev, preferred_element_type=jnp.float32)
        row_dot = jnp.einsum("tgd,gtd->gt", grad_head.astype(jnp.float32), output)
        dprob_own = jnp.einsum(
            "tgd,sd->gts", grad_head, value_own, preferred_element_type=jnp.float32
        )
        dprob_prev = jnp.einsum(
            "tgd,sd->gts", grad_head, value_prev, preferred_element_type=jnp.float32
        )
        dscore_own = (weight_own * (dprob_own - row_dot[:, :, None])).astype(jnp.bfloat16)
        dscore_prev = (weight_prev * (dprob_prev - row_dot[:, :, None])).astype(jnp.bfloat16)
        query_grad = (
            jnp.einsum("gts,sd->tgd", dscore_own, key_own, preferred_element_type=jnp.float32)
            + jnp.einsum("gts,sd->tgd", dscore_prev, key_prev, preferred_element_type=jnp.float32)
        ) * factor
        key_grad_own = (
            jnp.einsum("gts,tgd->sd", dscore_own, query_head, preferred_element_type=jnp.float32)
            * factor
        )
        key_grad_prev = (
            jnp.einsum("gts,tgd->sd", dscore_prev, query_head, preferred_element_type=jnp.float32)
            * factor
        )
        value_grad_own = jnp.einsum(
            "gts,tgd->sd", rounded_own, grad_head, preferred_element_type=jnp.float32
        )
        value_grad_prev = jnp.einsum(
            "gts,tgd->sd", rounded_prev, grad_head, preferred_element_type=jnp.float32
        )
        return (query_grad, key_grad_own, value_grad_own, key_grad_prev, value_grad_prev)

    stacked = (
        jnp.moveaxis(queries, 1, 0),
        jnp.moveaxis(grads_out, 1, 0),
        jnp.moveaxis(own_keys, 1, 0),
        jnp.moveaxis(own_values, 1, 0),
        jnp.moveaxis(prev_keys, 1, 0),
        jnp.moveaxis(prev_values, 1, 0),
    )
    results = lax.map(per_head, stacked)
    query_grad = jnp.moveaxis(results[0], 0, 1).reshape(query_matrix, -1)
    others = tuple((jnp.moveaxis(member, 0, 1).reshape(1, 1, length, -1) for member in results[1:]))
    return (query_grad,) + others


def on_device(query, dout, key_mant, value_mantissas, key_exps, value_exponents, reach):
    heads_per_group = QUERY_HEADS // KEY_VALUE_HEADS
    key_scales = jnp.exp2(key_exps.astype(jnp.float32)).astype(jnp.bfloat16)
    value_scales = jnp.exp2(value_exponents.astype(jnp.float32)).astype(jnp.bfloat16)
    previous = passed_along((key_mant, value_mantissas, key_scales, value_scales), "inner", 1)
    first_cycle = lax.axis_index("inner") == 0
    reach_rows = reach[0, 0]
    query_heads, grad_heads = (
        lax.all_to_all(query, "head", split_axis=3, concat_axis=2, tiled=True),
        lax.all_to_all(dout, "head", split_axis=3, concat_axis=2, tiled=True),
    )
    length = query_heads.shape[2]
    head_count = key_mant.shape[3] // HEAD_SIZE
    queries = query_heads.reshape(length, head_count, heads_per_group, HEAD_SIZE)
    grads_out = grad_heads.reshape(length, head_count, heads_per_group, HEAD_SIZE)
    own_keys = expand(key_mant[0, 0], key_scales[0, 0])
    own_values = expand(value_mantissas[0, 0], value_scales[0, 0])
    prev_keys = expand(previous[0][0, 0], previous[2][0, 0])
    prev_values = expand(previous[1][0, 0], previous[3][0, 0])
    query_grad, key_own, value_own, key_next, value_next = attend(
        queries, grads_out, own_keys, own_values, prev_keys, prev_values, first_cycle, reach_rows
    )
    rounded = query_grad.astype(jnp.bfloat16).reshape(1, 1, length, -1)
    query_out = lax.all_to_all(rounded, "head", split_axis=2, concat_axis=3, tiled=True)
    returned = passed_along(
        (key_next.astype(jnp.bfloat16), value_next.astype(jnp.bfloat16)), "inner", -1
    )
    key_grad = (key_own + returned[0].astype(jnp.float32)).astype(jnp.bfloat16)
    value_grad = (value_own + returned[1].astype(jnp.float32)).astype(jnp.bfloat16)
    return (query_out, key_grad, value_grad)


def solution(mesh):
    placed = (
        P("outer", "inner", "head", None),
        P("outer", "inner", "head", None),
        P("outer", "inner", None, "head"),
        P("outer", "inner", None, "head"),
        P("outer", "inner", None, "head"),
        P("outer", "inner", None, "head"),
        P("outer", "inner"),
    )
    return jax.shard_map(
        on_device,
        mesh=mesh,
        in_specs=placed,
        out_specs=(
            P("outer", "inner", "head", None),
            P("outer", "inner", None, "head"),
            P("outer", "inner", None, "head"),
        ),
        check_vma=False,
    )
```

profile of v0, /device:TPU:1, one launch (start us, length us, event | category | flops | bytes accessed | tf_op | source)
XLA Modules:
  0.0 171.1 jit_solution(7470694419550584133)
XLA Ops:
  1.3 4.6 %collective-permute-start.3 = (bf16[1,1,2,2]{3,2,1,0:T(2,128)(2,1)S(1)}, bf16[1,1,2,2]{3,2,1,0:T(2,128)(2,1)S(1)}, u32[]{:S(2)}, u32[]{:S(2)}) collective-permute-start(bf16[1,1,2,2]{3,2,1,0:T(2,128)(2,1)S(1)} %exponential_convert_fusion), channel_id=1, source_target_pairs={{0,16},{16,32},{32,48},{48,64},{64,80},{80,96},{96,112},{112,128},... | collective-permute-start | bytes 32 | tf_op jit(solution)/shard_map/ppermute | solution.py:17
  6.6 1.9 %collective-permute-start.1 = (bf16[1,1,2,2]{3,2,1,0:T(2,128)(2,1)S(1)}, bf16[1,1,2,2]{3,2,1,0:T(2,128)(2,1)S(1)}, u32[]{:S(2)}, u32[]{:S(2)}) collective-permute-start(bf16[1,1,2,2]{3,2,1,0:T(2,128)(2,1)S(1)} %exponential_convert_fusion.1), channel_id=1, source_target_pairs={{0,16},{16,32},{32,48},{48,64},{64,80},{80,96},{96,112},{112,128},... | collective-permute-start | bytes 32 | tf_op jit(solution)/shard_map/ppermute | solution.py:17
  8.5 1.7 copy.119
  10.2 3.4 %collective-permute-start.2 = (bf16[1,1,256,256]{2,3,1,0:T(8,128)(2,1)}, bf16[1,1,256,256]{2,3,1,0:T(8,128)(2,1)}, u32[]{:S(2)}, u32[]{:S(2)}) collective-permute-start(bf16[1,1,256,256]{2,3,1,0:T(8,128)(2,1)} %copy.119), channel_id=1, source_target_pairs={{0,16},{16,32},{32,48},{48,64},{64,80},{80,96},{96,112},{112,128},... | collective-permute-start | bytes 393224 | tf_op jit(solution)/shard_map/ppermute | solution.py:17
  13.6 1.7 copy.113
  15.2 1.9 %collective-permute-start = (bf16[1,1,256,256]{2,3,1,0:T(8,128)(2,1)}, bf16[1,1,256,256]{2,3,1,0:T(8,128)(2,1)}, u32[]{:S(2)}, u32[]{:S(2)}) collective-permute-start(bf16[1,1,256,256]{2,3,1,0:T(8,128)(2,1)} %copy.113), channel_id=1, source_target_pairs={{0,16},{16,32},{32,48},{48,64},{64,80},{80,96},{96,112},{112,128},... | collective-permute-start | bytes 393224 | tf_op jit(solution)/shard_map/ppermute | solution.py:17
  17.1 5.0 %copy.115 = bf16[1,1,128,4096]{2,1,0,3:T(2,128)(2,1)S(1)} copy(bf16[1,1,128,4096]{3,2,1,0:T(8,128)(2,1)} %param.9) | data formatting | bytes 2097152 | tf_op args[0]
  22.8 22.4 %reduce.2 = bf16[4096,128]{1,0:T(8,128)(2,1)S(1)} reduce(bf16[4096,1,1,128]{3,2,1,0:T(2,128)(2,1)S(1)} %bitcast.306, bf16[]{:T(256)} %broadcast.60), dimensions={1,2}, to_apply=%bitcast.201.reduce_sub_computation | reduce | bytes 2097154
  46.4 4.2 %all-to-all-start = ((bf16[2,2,131072]{2,1,0:T(2,128)(2,1)}), bf16[2,2,131072]{2,1,0:T(2,128)(2,1)S(1)}, u32[]{:S(2)}, u32[]{:S(2)}) async-start(bf16[2,2,131072]{2,1,0:T(2,128)(2,1)} %reshape.109), calls=%async_computation | async-start | bytes 2097152 | tf_op jit(solution)/shard_map/all_to_all | solution.py:116
  51.7 5.0 %copy.121 = bf16[1,1,128,4096]{2,1,0,3:T(2,128)(2,1)S(1)} copy(bf16[1,1,128,4096]{3,2,1,0:T(8,128)(2,1)} %param.10) | data formatting | bytes 2097152 | tf_op args[1]
  56.7 23.4 %reduce.3 = bf16[4096,128]{1,0:T(8,128)(2,1)} reduce(bf16[4096,1,1,128]{3,2,1,0:T(2,128)(2,1)S(1)} %bitcast.308, bf16[]{:T(256)} %broadcast.60), dimensions={1,2}, to_apply=%bitcast.203.reduce_sub_computation | reduce | bytes 2097154
  80.1 2.2 %reshape.111 = bf16[2,2,131072]{2,1,0:T(2,128)(2,1)} reshape(bf16[4096,128]{1,0:T(8,128)(2,1)} %reduce.3) | data formatting | bytes 2097152
  83.6 4.6 %all-to-all-start.1 = ((bf16[2,2,131072]{2,1,0:T(2,128)(2,1)}), bf16[2,2,131072]{2,1,0:T(2,128)(2,1)}, u32[]{:S(2)}, u32[]{:S(2)}) async-start(bf16[2,2,131072]{2,1,0:T(2,128)(2,1)} %reshape.111), calls=%async_computation.1 | async-start | bytes 2097152 | tf_op jit(solution)/shard_map/all_to_all | solution.py:117
  88.3 1.6 multiply_bitcast_fusion
  92.6 9.1 %all-to-all-done.1 = bf16[2,2,131072]{2,1,0:T(2,128)(2,1)} async-done(((bf16[2,2,131072]{2,1,0:T(2,128)(2,1)}), bf16[2,2,131072]{2,1,0:T(2,128)(2,1)}, u32[]{:S(2)}, u32[]{:S(2)}) %all-to-all-start.1) | async-done | bytes 1048608 | tf_op jit(solution)/shard_map/all_to_all | solution.py:117
  101.8 2.0 %reshape.112 = bf16[4096,1,1,128]{3,2,1,0:T(2,128)(2,1)S(1)} reshape(bf16[2,2,131072]{2,1,0:T(2,128)(2,1)} %all-to-all-done.1) | data formatting | bytes 2097152
  106.6 21.6 %while.19 = (s32[]{:T(128)}, bf16[2,256,8,128]{1,3,2,0:T(8,128)(2,1)}, f32[2,256,128]{2,1,0:T(8,128)}, f32[2,256,128]{2,1,0:T(8,128)}, bf16[2,256,128]{2,1,0:T(8...) while((s32[]{:T(128)}, ...), condition=%wide.region_5.6_spmd.clone, body=%wide.region_0.5_spmd.clone.sunk | while | flops 1631709696 | bytes 56954876 | solution.py:102
  129.3 4.7 %collective-permute-start.4 = (bf16[1,1,256,256]{3,2,1,0:T(8,128)(2,1)S(1)}, bf16[1,1,256,256]{3,2,1,0:T(8,128)(2,1)S(1)}, u32[]{:S(2)}, u32[]{:S(2)}) collective-permute-start(bf16[1,1,256,256]{3,2,1,0:T(8,128)(2,1)S(1)} %convert_element_type.96), channel_id=1, source_target_pairs={{16,0},{32,16},{48,32},{64,48},{80,64},{96,80},{112,96},{128,112},... | collective-permute-start | bytes 393224 | tf_op jit(solution)/shard_map/ppermute | solution.py:17
  133.9 4.8 %copy.131 = bf16[1,1,256,2048]{3,1,0,2:T(2,128)(2,1)S(1)} copy(bf16[1,1,256,2048]{2,3,1,0:T(8,128)(2,1)} %bitcast.315) | data formatting | bytes 2097152 | tf_op jit(solution)/shard_map/convert_element_type | solution.py:130
  138.7 6.8 %reduce.4 = bf16[256,2048]{1,0:T(8,128)(2,1)S(1)} reduce(bf16[256,1,1,2048]{3,2,1,0:T(2,128)(2,1)S(1)} %bitcast.307, bf16[]{:T(256)} %broadcast.60), dimensions={1,2}, to_apply=%bitcast.205.reduce_sub_computation | reduce | bytes 2097154
  145.6 1.6 reshape.113
  147.1 3.7 %all-to-all-start.2 = ((bf16[2,2,131072]{2,1,0:T(2,128)(2,1)}), bf16[2,2,131072]{2,1,0:T(2,128)(2,1)S(1)}, u32[]{:S(2)}, u32[]{:S(2)}) async-start(bf16[2,2,131072]{2,1,0:T(2,128)(2,1)} %reshape.113), calls=%async_computation.2 | async-start | bytes 2097152 | tf_op jit(solution)/shard_map/all_to_all | solution.py:131
  151.1 1.9 %collective-permute-start.5 = (bf16[1,1,256,256]{3,2,1,0:T(8,128)(2,1)S(1)}, bf16[1,1,256,256]{3,2,1,0:T(8,128)(2,1)S(1)}, u32[]{:S(2)}, u32[]{:S(2)}) collective-permute-start(bf16[1,1,256,256]{3,2,1,0:T(8,128)(2,1)S(1)} %convert_element_type.101), channel_id=1, source_target_pairs={{16,0},{32,16},{48,32},{64,48},{80,64},{96,80},{112,96},{128,112},... | collective-permute-start | bytes 393224 | tf_op jit(solution)/shard_map/ppermute | solution.py:17
  154.6 11.0 %collective-permute-done.5 = bf16[1,1,256,256]{3,2,1,0:T(8,128)(2,1)S(1)} collective-permute-done((bf16[1,1,256,256]{3,2,1,0:T(8,128)(2,1)S(1)}, bf16[1,1,256,256]{3,2,1,0:T(8,128)(2,1)S(1)}, u32[]{:S(2)}, u32[]{:S(2)}) %collective-permute-start.5) | collective-permute-done | bytes 131104 | tf_op jit(solution)/shard_map/ppermute | solution.py:17
  (145 shorter events, 39.9 us)
Async XLA Ops:
  1.3 81.9 %collective-permute-start.3 = (bf16[1,1,2,2]{3,2,1,0:T(2,128)(2,1)S(1)}, bf16[1,1,2,2]{3,2,1,0:T(2,128)(2,1)S(1)}, u32[]{:S(2)}, u32[]{:S(2)}) collective-permute-start(bf16[1,1,2,2]{3,2,1,0:T(2,128)(2,1)S(1)} %exponential_convert_fusion), channel_id=1, source_target_pairs={{0,16},{16,32},{32,48},{48,64},{64,80},{80,96},{96,112},{112,128},... | collective-permute-start | bytes 32 | tf_op jit(solution)/shard_map/ppermute | solution.py:17
  6.6 76.8 %collective-permute-start.1 = (bf16[1,1,2,2]{3,2,1,0:T(2,128)(2,1)S(1)}, bf16[1,1,2,2]{3,2,1,0:T(2,128)(2,1)S(1)}, u32[]{:S(2)}, u32[]{:S(2)}) collective-permute-start(bf16[1,1,2,2]{3,2,1,0:T(2,128)(2,1)S(1)} %exponential_convert_fusion.1), channel_id=1, source_target_pairs={{0,16},{16,32},{32,48},{48,64},{64,80},{80,96},{96,112},{112,128},... | collective-permute-start | bytes 32 | tf_op jit(solution)/shard_map/ppermute | solution.py:17
  10.2 78.1 %collective-permute-start.2 = (bf16[1,1,256,256]{2,3,1,0:T(8,128)(2,1)}, bf16[1,1,256,256]{2,3,1,0:T(8,128)(2,1)}, u32[]{:S(2)}, u32[]{:S(2)}) collective-permute-start(bf16[1,1,256,256]{2,3,1,0:T(8,128)(2,1)} %copy.119), channel_id=1, source_target_pairs={{0,16},{16,32},{32,48},{48,64},{64,80},{80,96},{96,112},{112,128},... | collective-permute-start | bytes 393224 | tf_op jit(solution)/shard_map/ppermute | solution.py:17
  15.2 74.6 %collective-permute-start = (bf16[1,1,256,256]{2,3,1,0:T(8,128)(2,1)}, bf16[1,1,256,256]{2,3,1,0:T(8,128)(2,1)}, u32[]{:S(2)}, u32[]{:S(2)}) collective-permute-start(bf16[1,1,256,256]{2,3,1,0:T(8,128)(2,1)} %copy.113), channel_id=1, source_target_pairs={{0,16},{16,32},{32,48},{48,64},{64,80},{80,96},{96,112},{112,128},... | collective-permute-start | bytes 393224 | tf_op jit(solution)/shard_map/ppermute | solution.py:17
  45.2 5.4 %copy-start.14 = (s32[1,1,2,2]{3,2,1,0:T(2,128)S(1)}, s32[1,1,2,2]{3,2,1,0:T(2,128)}, u32[]{:S(2)}) copy-start(s32[1,1,2,2]{3,2,1,0:T(2,128)} %param.13) | copy-start | bytes 52
  45.2 5.4 %copy-start.15 = (s32[1,1,2,2]{3,2,1,0:T(2,128)S(1)}, s32[1,1,2,2]{3,2,1,0:T(2,128)}, u32[]{:S(2)}) copy-start(s32[1,1,2,2]{3,2,1,0:T(2,128)} %param.14) | copy-start | bytes 52
  46.4 37.2 %all-to-all-start = ((bf16[2,2,131072]{2,1,0:T(2,128)(2,1)}), bf16[2,2,131072]{2,1,0:T(2,128)(2,1)S(1)}, u32[]{:S(2)}, u32[]{:S(2)}) async-start(bf16[2,2,131072]{2,1,0:T(2,128)(2,1)} %reshape.109), calls=%async_computation | async-start | bytes 2097152 | tf_op jit(solution)/shard_map/all_to_all | solution.py:116
  83.6 18.2 %all-to-all-start.1 = ((bf16[2,2,131072]{2,1,0:T(2,128)(2,1)}), bf16[2,2,131072]{2,1,0:T(2,128)(2,1)}, u32[]{:S(2)}, u32[]{:S(2)}) async-start(bf16[2,2,131072]{2,1,0:T(2,128)(2,1)} %reshape.111), calls=%async_computation.1 | async-start | bytes 2097152 | tf_op jit(solution)/shard_map/all_to_all | solution.py:117
  109.5 1.4 copy-start.10
  110.9 1.5 copy-start.3
  113.4 1.4 copy-start.5
  114.7 1.6 copy-start.13
  114.8 1.3 copy-start
  120.2 1.4 copy-start.10
  121.7 1.5 copy-start.3
  124.1 1.4 copy-start.5
  125.5 1.6 copy-start.13
  125.5 1.3 copy-start
  129.3 24.7 %collective-permute-start.4 = (bf16[1,1,256,256]{3,2,1,0:T(8,128)(2,1)S(1)}, bf16[1,1,256,256]{3,2,1,0:T(8,128)(2,1)S(1)}, u32[]{:S(2)}, u32[]{:S(2)}) collective-permute-start(bf16[1,1,256,256]{3,2,1,0:T(8,128)(2,1)S(1)} %convert_element_type.96), channel_id=1, source_target_pairs={{16,0},{32,16},{48,32},{64,48},{80,64},{96,80},{112,96},{128,112},... | collective-permute-start | bytes 393224 | tf_op jit(solution)/shard_map/ppermute | solution.py:17
  145.5 5.3 %copy-start.11 = (bf16[2,256,128]{2,1,0:T(8,128)(2,1)S(1)}, bf16[2,256,128]{2,1,0:T(8,128)(2,1)}, u32[]{:S(2)}) copy-start(bf16[2,256,128]{2,1,0:T(8,128)(2,1)} %get-tuple-element.83) | copy-start | bytes 393220
  145.5 7.5 %copy-start.7 = (f32[2,256,128]{2,1,0:T(8,128)S(1)}, f32[2,256,128]{2,1,0:T(8,128)}, u32[]{:S(2)}) copy-start(f32[2,256,128]{2,1,0:T(8,128)} %get-tuple-element.80) | copy-start | bytes 786436
  147.1 6.3 %copy-start.4 = (f32[2,256,128]{2,1,0:T(8,128)S(1)}, f32[2,256,128]{2,1,0:T(8,128)}, u32[]{:S(2)}) copy-start(f32[2,256,128]{2,1,0:T(8,128)} %get-tuple-element.82) | copy-start | bytes 786436
  147.1 20.4 %all-to-all-start.2 = ((bf16[2,2,131072]{2,1,0:T(2,128)(2,1)}), bf16[2,2,131072]{2,1,0:T(2,128)(2,1)S(1)}, u32[]{:S(2)}, u32[]{:S(2)}) async-start(bf16[2,2,131072]{2,1,0:T(2,128)(2,1)} %reshape.113), calls=%async_computation.2 | async-start | bytes 2097152 | tf_op jit(solution)/shard_map/all_to_all | solution.py:131
  151.1 14.5 %collective-permute-start.5 = (bf16[1,1,256,256]{3,2,1,0:T(8,128)(2,1)S(1)}, bf16[1,1,256,256]{3,2,1,0:T(8,128)(2,1)S(1)}, u32[]{:S(2)}, u32[]{:S(2)}) collective-permute-start(bf16[1,1,256,256]{3,2,1,0:T(8,128)(2,1)S(1)} %convert_element_type.101), channel_id=1, source_target_pairs={{16,0},{32,16},{48,32},{64,48},{80,64},{96,80},{112,96},{128,112},... | collective-permute-start | bytes 393224 | tf_op jit(solution)/shard_map/ppermute | solution.py:17
  (12 other events, 11.8 us)
where the time goes:
time: 172 us; the launch traced here: 171 us
  other arithmetic  61.2 us (36%)
  local copies, waits for them, and re-layouts  41.8 us (24%)
  starting transfers between devices  30.9 us (18%)
  waiting for transfers between devices  21.4 us (12%)
  matrix products  13.6 us (8%)
    unnamed x3, other arithmetic  52.7 us
    unnamed x35, local copies, waits for them, and re-layouts  26.6 us
    ppermute x6, starting transfers between devices, passed_along(): lax.ppermute(value, axis, [(source, source + steps) for source in range(i...  18.4 us
    ppermute x6, waiting for transfers between devices, passed_along(): lax.ppermute(value, axis, [(source, source + steps) for source in range(i...  11 us
    all_to_all x1, waiting for transfers between devices, on_device(): lax.all_to_all(dout, 'head', split_axis=3, concat_axis=2, tiled=True)  9.11 us
    while x44, local copies, waits for them, and re-layouts  4.99 us
    convert_element_type x1, local copies, waits for them, and re-layouts, on_device(): rounded = query_grad.astype(jnp.bfloat16).reshape(1, 1, length, -1)  4.75 us
    all_to_all x1, starting transfers between devices, on_device(): lax.all_to_all(dout, 'head', split_axis=3, concat_axis=2, tiled=True)  4.64 us
  transfers between devices with their start and end apart: 9, of which 3 were waited for; matrix products, arithmetic and copies ran while one was open for 50% of the time, Pallas kernels for 0%

commit v1 on v0

v1 whole, which is shorter than its diff:
```python
import functools

import jax
import jax.numpy as jnp
from jax import lax
from jax.experimental import pallas as pl
from jax.experimental.pallas import tpu as pltpu
from jax.sharding import PartitionSpec as P

QUERY_HEADS = 32
KEY_VALUE_HEADS = 4
HEAD_SIZE = 128
ROWS_PER_SCALE = 128
GROUP = QUERY_HEADS // KEY_VALUE_HEADS
FACTOR = HEAD_SIZE**-0.5
LOG2_E = 1.4426950408889634
NEG_FILL = -1e30
PAIR = 2


def nt(a, b):
    return lax.dot_general(a, b, (((1,), (1,)), ((), ())), preferred_element_type=jnp.float32)


def nn(a, b):
    return lax.dot_general(a, b, (((1,), (0,)), ((), ())), preferred_element_type=jnp.float32)


def pack_kernel(key_exps, value_exps, key_ref, value_ref, out_ref):
    length = key_ref.shape[0]
    for source, exps, base in ((key_ref, key_exps, 0), (value_ref, value_exps, length)):
        for run in range(length // ROWS_PER_SCALE):
            rows = slice(run * ROWS_PER_SCALE, (run + 1) * ROWS_PER_SCALE)
            for head in range(source.shape[1] // HEAD_SIZE):
                cols = slice(head * HEAD_SIZE, (head + 1) * HEAD_SIZE)
                exponent = jnp.full((8, HEAD_SIZE), exps[run, head], jnp.int32).astype(jnp.float32)
                scale = jnp.exp2(exponent)[:1]
                out_ref[base + run * ROWS_PER_SCALE : base + (run + 1) * ROWS_PER_SCALE, cols] = (
                    source[rows, cols].astype(jnp.float32) * scale
                ).astype(jnp.bfloat16)


def pack(key_mant, value_mant, key_exps, value_exps):
    length, width = key_mant.shape
    smem = pl.BlockSpec(memory_space=pltpu.SMEM)
    vmem = pl.BlockSpec(memory_space=pltpu.VMEM)
    return pl.pallas_call(
        pack_kernel,
        out_shape=jax.ShapeDtypeStruct((2 * length, width), jnp.bfloat16),
        in_specs=[smem, smem, vmem, vmem],
        out_specs=vmem,
        name="pack",
    )(key_exps, value_exps, key_mant, value_mant)


def attend_kernel(place, q_ref, g_ref, own_ref, prev_ref, *refs):
    dq_ref, next_ref, term_ref = refs[-3:]
    tokens = q_ref.shape[0]
    length = own_ref.shape[0] // 2
    rows = lax.broadcasted_iota(jnp.int32, (2 * length, tokens), 0)
    cols = lax.broadcasted_iota(jnp.int32, (2 * length, tokens), 1)
    last = jnp.where(rows < length, 2 * length, cols + (length + place[1] * tokens))
    visible = jnp.logical_and(rows >= place[2], rows <= last)
    bias = jnp.where(visible, 0.0, NEG_FILL)
    bias = jnp.concatenate([bias] * PAIR, axis=1)
    keys = jnp.concatenate([prev_ref[:length], own_ref[:length]], axis=0)
    values = jnp.concatenate([prev_ref[length:], own_ref[length:]], axis=0)
    keys_t = keys.T
    dk = dv = None
    for start in range(0, GROUP, PAIR):
        spans = [slice(h * HEAD_SIZE, (h + 1) * HEAD_SIZE) for h in range(start, start + PAIR)]
        queries = jnp.concatenate([q_ref[:, s] for s in spans], axis=0)
        grads = jnp.concatenate([g_ref[:, s] for s in spans], axis=0)
        scores = nt(keys, queries) + bias
        dprob = nt(values, grads)
        peak = jnp.max(scores, axis=0, keepdims=True)
        weights = jnp.exp2((scores - peak) * (FACTOR * LOG2_E))
        inverse = 1.0 / jnp.sum(weights, axis=0, keepdims=True)
        row_dot = jnp.sum(weights * dprob, axis=0, keepdims=True) * inverse
        probs = weights * inverse
        dscore = (probs * (dprob - row_dot)).astype(jnp.bfloat16)
        probs = probs.astype(jnp.bfloat16)
        dk_part = nn(dscore, queries)
        dv_part = nn(probs, grads)
        dk = dk_part if dk is None else dk + dk_part
        dv = dv_part if dv is None else dv + dv_part
        dq = (nn(keys_t, dscore) * FACTOR).astype(jnp.bfloat16).T
        for at, s in enumerate(spans):
            dq_ref[:, s] = dq[at * tokens : (at + 1) * tokens]
    dk = dk * FACTOR
    next_ref[:length] = dk[:length].astype(next_ref.dtype)
    next_ref[length:] = dv[:length].astype(next_ref.dtype)
    term_ref[:length] = dk[length:].astype(term_ref.dtype)
    term_ref[length:] = dv[length:].astype(term_ref.dtype)


def attend(place, query, dout, own, prev, dq_so_far, term_dtype, name):
    tokens, width = query.shape
    rows, half = own.shape
    heads = half // HEAD_SIZE
    wide = pl.BlockSpec((tokens, GROUP * HEAD_SIZE), lambda j, s: (0, heads * s[0] + j))
    narrow = pl.BlockSpec((rows, HEAD_SIZE), lambda j, s: (0, j))
    operands = [place, query, dout, own, prev]
    in_specs = [wide, wide, narrow, narrow]
    aliases = {}
    if dq_so_far is not None:
        operands.append(dq_so_far)
        in_specs.append(pl.BlockSpec(memory_space=pl.ANY))
        aliases = {5: 0}
    return pl.pallas_call(
        attend_kernel,
        out_shape=(
            jax.ShapeDtypeStruct((tokens, width), jnp.bfloat16),
            jax.ShapeDtypeStruct((rows, half), jnp.bfloat16),
            jax.ShapeDtypeStruct((rows, half), term_dtype),
        ),
        grid_spec=pltpu.PrefetchScalarGridSpec(
            num_scalar_prefetch=1,
            grid=(heads,),
            in_specs=in_specs,
            out_specs=[wide, narrow, narrow],
        ),
        input_output_aliases=aliases,
        cost_estimate=pl.CostEstimate(
            flops=10 * heads * GROUP * tokens * rows * HEAD_SIZE,
            bytes_accessed=4 * 1024 * 1024,
            transcendentals=heads * GROUP * tokens * rows,
        ),
        compiler_params=pltpu.CompilerParams(vmem_limit_bytes=32 * 1024 * 1024),
        name=name,
    )(*operands)


def on_device(query, dout, key_mant, value_mantissas, key_exps, value_exponents, reach):
    inner = lax.axis_size("inner")
    mine = lax.axis_index("head")
    first = lax.axis_index("inner") == 0
    length = key_mant.shape[2]
    query_rows, dout_rows = query[0, 0], dout[0, 0]
    own = pack(key_mant[0, 0], value_mantissas[0, 0], key_exps[0, 0], value_exponents[0, 0])

    def forward(value):
        return lax.ppermute(value, "inner", [(i, i + 1) for i in range(inner - 1)])

    def backward(value):
        return lax.ppermute(value, "inner", [(i + 1, i) for i in range(inner - 1)])

    def swap(value):
        return lax.ppermute(value, "head", [(0, 1), (1, 0)])

    def across(value, step):
        pairs = [
            (head * inner + at, (1 - head) * inner + at + step)
            for head in range(2)
            for at in range(max(0, -step), min(inner, inner - step))
        ]
        return lax.ppermute(value, ("head", "inner"), pairs)

    prev = forward(own)
    other_own = swap(own)
    other_prev = across(own, 1)
    lowest = jnp.where(first, length, length - reach[0, 0])
    local = jnp.stack([mine, mine, lowest]).astype(jnp.int32)
    remote = jnp.stack([1 - mine, mine, lowest]).astype(jnp.int32)
    dq, next_here, term_here = attend(
        local, query_rows, dout_rows, own, prev, None, jnp.float32, "attend_local"
    )
    returned = backward(next_here)
    dq, next_there, term_there = attend(
        remote, query_rows, dout_rows, other_own, other_prev, dq, jnp.bfloat16, "attend_remote"
    )
    swapped = swap(term_there)
    crossed = across(next_there, -1)
    total = term_here
    for part in (returned, swapped, crossed):
        total = total + part.astype(jnp.float32)
    total = total.astype(jnp.bfloat16)
    return dq[None, None], total[None, None, :length], total[None, None, length:]


def solution(mesh):
    placed = (
        P("outer", "inner", "head", None),
        P("outer", "inner", "head", None),
        P("outer", "inner", None, "head"),
        P("outer", "inner", None, "head"),
        P("outer", "inner", None, "head"),
        P("outer", "inner", None, "head"),
        P("outer", "inner"),
    )
    return jax.shard_map(
        on_device,
        mesh=mesh,
        in_specs=placed,
        out_specs=(
            P("outer", "inner", "head", None),
            P("outer", "inner", None, "head"),
            P("outer", "inner", None, "head"),
        ),
        check_vma=False,
    )
```

time: 172 us -> 49.7 us (0.29)
  other arithmetic: 61.2 us -> 0.27 us
  local copies, waits for them, and re-layouts: 41.8 us -> 4.12 us
  Pallas kernels: 0 us -> 15 us
  waiting for transfers between devices: 21.4 us -> 7.64 us
  matrix products: 13.6 us -> 0 us
  starting transfers between devices: 30.9 us -> 20.9 us
    unnamed x3 -> x0, other arithmetic: 52.7 us -> none
    unnamed x35 -> x6, local copies, waits for them, and re-layouts: 26.6 us -> 3.4 us
    pallas_call x0 -> x3, Pallas kernels: none -> 15 us  [the longest x2 13.3 us: attend(): pl.pallas_call(attend_kernel, out_shape=(jax.ShapeDtypeStruct((tokens, wi...]
    dot_general x24 -> x0, matrix products: 13.6 us -> none  [the longest x2 2.03 us: per_head(): jnp.einsum('gts,sd->gtd', rounded_prev, value_prev, preferred_element_typ...]
    all_to_all x3 -> x0, starting transfers between devices: 12.5 us -> none  [the longest x1 4.64 us: on_device(): lax.all_to_all(dout, 'head', split_axis=3, concat_axis=2, tiled=True)]
    all_to_all x3 -> x0, waiting for transfers between devices: 10.4 us -> none  [the longest x1 9.11 us: on_device(): lax.all_to_all(dout, 'head', split_axis=3, concat_axis=2, tiled=True)]
    convert_element_type x5 -> x0, local copies, waits for them, and re-layouts: 6.11 us -> none  [the longest x1 4.75 us: on_device(): rounded = query_grad.astype(jnp.bfloat16).reshape(1, 1, length, -1)]
    while x44 -> x0, local copies, waits for them, and re-layouts: 4.99 us -> none
  transfers between devices with their start and end apart: 9 -> 6, of which waited for: 3 -> 3; matrix products, arithmetic and copies ran while one was open for 50% -> 0% of each run, Pallas kernels for 0% -> 13%
where the time goes in v1:
time: 49.7 us; the launch traced here: 49.3 us
  starting transfers between devices  20.9 us (42%)
  Pallas kernels  15 us (30%)
  waiting for transfers between devices  7.64 us (15%)
  local copies, waits for them, and re-layouts  4.12 us (8%)
  between operations  1.35 us (3%)
    pallas_call x2, Pallas kernels, attend(): pl.pallas_call(attend_kernel, out_shape=(jax.ShapeDtypeStruct((tokens, wi...  13.3 us
    ppermute x2, starting transfers between devices, across(): return lax.ppermute(value, ('head', 'inner'), pairs)  7.64 us
    ppermute x2, waiting for transfers between devices, across(): return lax.ppermute(value, ('head', 'inner'), pairs)  6.88 us
    ppermute x2, starting transfers between devices, swap(): return lax.ppermute(value, 'head', [(0, 1), (1, 0)])  6.77 us
    ppermute x1, starting transfers between devices, forward(): return lax.ppermute(value, 'inner', [(i, i + 1) for i in range(inner - 1)])  4.58 us
    unnamed x6, local copies, waits for them, and re-layouts  3.4 us
    ppermute x1, starting transfers between devices, backward(): return lax.ppermute(value, 'inner', [(i + 1, i) for i in range(inner - 1)])  1.92 us
    pallas_call x1, Pallas kernels, pack(): pl.pallas_call(pack_kernel, out_shape=jax.ShapeDtypeStruct((2 * length, w...  1.76 us
  transfers between devices with their start and end apart: 6, of which 3 were waited for; matrix products, arithmetic and copies ran while one was open for 0% of the time, Pallas kernels for 13%

profile of v1, /device:TPU:1, one launch (start us, length us, event | category | flops | bytes accessed | tf_op | source)
XLA Modules:
  0.0 49.3 jit_solution(3996404211944787119)
XLA Ops:
  0.6 1.8 %pack.1.own_ref = bf16[512,256]{1,0:T(8,128)(2,1)} custom-call(s32[2,2]{1,0:T(2,128)} %bitcast.21, s32[2,2]{1,0:T(2,128)} %bitcast.22, bf16[256,256]{1,0:T(8,128)(2,1)} %bitcast.19, bf16[256,256]{1,0:T(8,128)(2,1)} %bitcast.20), custom_call_target="tpu_custom_call" | custom-call | tf_op jit(solution)/shard_map/pack/pallas_call | solution.py:47
  2.4 4.6 %collective-permute-start.2 = (bf16[512,256]{1,0:T(8,128)(2,1)}, bf16[512,256]{1,0:T(8,128)(2,1)S(1)}, u32[]{:S(2)}, u32[]{:S(2)}) collective-permute-start(bf16[512,256]{1,0:T(8,128)(2,1)} %pack.1.own_ref), channel_id=1, source_target_pairs={{0,16},{16,32},{32,48},{48,64},{64,80},{80,96},{96,112},{112,128},... | collective-permute-start | bytes 786440 | tf_op jit(solution)/shard_map/ppermute | solution.py:143
  7.0 3.4 %collective-permute-start.1 = (bf16[512,256]{1,0:T(8,128)(2,1)}, bf16[512,256]{1,0:T(8,128)(2,1)S(1)}, u32[]{:S(2)}, u32[]{:S(2)}) collective-permute-start(bf16[512,256]{1,0:T(8,128)(2,1)} %pack.1.own_ref), channel_id=1, source_target_pairs={{0,272},{16,288},{32,304},{48,320},{64,336},{80,352},{96,368},{112... | collective-permute-start | bytes 786440 | tf_op jit(solution)/shard_map/ppermute | solution.py:157
  10.3 3.1 %collective-permute-start = (bf16[512,256]{1,0:T(8,128)(2,1)}, bf16[512,256]{1,0:T(8,128)(2,1)S(1)}, u32[]{:S(2)}, u32[]{:S(2)}) collective-permute-start(bf16[512,256]{1,0:T(8,128)(2,1)} %pack.1.own_ref), channel_id=1, source_target_pairs={{0,256},{256,0},{1,257},{257,1},{2,258},{258,2},{3,259},{259,3},{4... | collective-permute-start | bytes 786440 | tf_op jit(solution)/shard_map/ppermute | solution.py:149
  14.1 0.1 add_add_fusion.1.place
  14.2 0.1 add_add_fusion.place
  14.3 0.0 collective-permute-done.2.prev_ref
  14.3 0.0 copy-start
  14.3 1.0 %copy-done = bf16[512,256]{1,0:T(8,128)(2,1)S(1)} copy-done((bf16[512,256]{1,0:T(8,128)(2,1)S(1)}, bf16[512,256]{1,0:T(8,128)(2,1)}, u32[]{:S(2)}) %copy-start) | copy-done | bytes 262168
  15.2 0.0 copy-start.1
  15.2 1.2 %copy-done.1 = bf16[1,1,128,4096]{3,2,1,0:T(8,128)(2,1)S(1)} copy-done((bf16[1,1,128,4096]{3,2,1,0:T(8,128)(2,1)S(1)}, bf16[1,1,128,4096]{3,2,1,0:T(8,128)(2,1)}, u32[]{:S(2)}) %copy-start.1) | copy-done | bytes 1048600
  16.4 1.2 %copy-done.2 = bf16[1,1,128,4096]{3,2,1,0:T(8,128)(2,1)S(1)} copy-done((bf16[1,1,128,4096]{3,2,1,0:T(8,128)(2,1)S(1)}, bf16[1,1,128,4096]{3,2,1,0:T(8,128)(2,1)}, u32[]{:S(2)}) %copy-start.2) | copy-done | bytes 1048600
  17.7 6.6 %attend_local.1 = (bf16[128,4096]{1,0:T(8,128)(2,1)}, bf16[512,256]{1,0:T(8,128)(2,1)S(1)}, f32[512,256]{1,0:T(8,128)S(1)}) custom-call(s32[3]{0:T(128)S(1)} %add_add_fusion.1.place, bf16[128,4096]{1,0:T(8,128)(2,1)S(1)} %bitcast.15, bf16[128,4096]{1,0:T(8,128)(2,1)S(1)} %bitcast.17, bf16[512,256]{1,0:T(8,128)(2,1)S(1)} %copy-done, ...), custom_call_target="tpu_custom_call" | custom-call | flops 1342177280 | bytes 4194304 | tf_op jit(solution)/shard_map/attend_local/pallas_call | solution.py:110
  24.3 0.0 collective-permute-done.1.prev_ref
  24.3 0.0 collective-permute-done.own_ref
  24.3 6.6 %attend_remote.1 = (bf16[128,4096]{1,0:T(8,128)(2,1)}, bf16[512,256]{1,0:T(8,128)(2,1)S(1)}, bf16[512,256]{1,0:T(8,128)(2,1)S(1)}) custom-call(s32[3]{0:T(128)S(1)} %add_add_fusion.place, bf16[128,4096]{1,0:T(8,128)(2,1)S(1)} %bitcast.16, bf16[128,4096]{1,0:T(8,128)(2,1)S(1)} %bitcast.18, ...), custom_call_target="tpu_custom_call", output_to_operand_aliasing={{0}: (5, {})} | custom-call | flops 1342177280 | bytes 4194304 | tf_op jit(solution)/shard_map/attend_remote/pallas_call | solution.py:110
  30.9 3.7 %collective-permute-start.4 = (bf16[512,256]{1,0:T(8,128)(2,1)S(1)}, bf16[512,256]{1,0:T(8,128)(2,1)S(1)}, u32[]{:S(2)}, u32[]{:S(2)}) collective-permute-start(bf16[512,256]{1,0:T(8,128)(2,1)S(1)} %get-tuple-element.13), channel_id=1, source_target_pairs={{0,256},{256,0},{1,257},{257,1},{2,258},{258,2},{3,259},{259,3},{4... | collective-permute-start | bytes 786440 | tf_op jit(solution)/shard_map/ppermute | solution.py:149
  34.6 4.3 %collective-permute-start.5 = (bf16[512,256]{1,0:T(8,128)(2,1)S(1)}, bf16[512,256]{1,0:T(8,128)(2,1)S(1)}, u32[]{:S(2)}, u32[]{:S(2)}) collective-permute-start(bf16[512,256]{1,0:T(8,128)(2,1)S(1)} %get-tuple-element.14), channel_id=1, source_target_pairs={{16,256},{32,272},{48,288},{64,304},{80,320},{96,336},{112,352},{1... | collective-permute-start | bytes 786440 | tf_op jit(solution)/shard_map/ppermute | solution.py:157
  38.9 1.9 %collective-permute-start.3 = (bf16[512,256]{1,0:T(8,128)(2,1)S(1)}, bf16[512,256]{1,0:T(8,128)(2,1)S(1)}, u32[]{:S(2)}, u32[]{:S(2)}) collective-permute-start(bf16[512,256]{1,0:T(8,128)(2,1)S(1)} %get-tuple-element.12), channel_id=1, source_target_pairs={{16,0},{32,16},{48,32},{64,48},{80,64},{96,80},{112,96},{128,112},... | collective-permute-start | bytes 786440 | tf_op jit(solution)/shard_map/ppermute | solution.py:146
  40.8 0.2 collective-permute-done.4
  41.1 6.9 %collective-permute-done.5 = bf16[512,256]{1,0:T(8,128)(2,1)S(1)} collective-permute-done((bf16[512,256]{1,0:T(8,128)(2,1)S(1)}, bf16[512,256]{1,0:T(8,128)(2,1)S(1)}, u32[]{:S(2)}, u32[]{:S(2)}) %collective-permute-start.5) | collective-permute-done | bytes 262176 | tf_op jit(solution)/shard_map/ppermute | solution.py:157
  48.0 0.5 %collective-permute-done.3 = bf16[512,256]{1,0:T(8,128)(2,1)S(1)} collective-permute-done((bf16[512,256]{1,0:T(8,128)(2,1)S(1)}, bf16[512,256]{1,0:T(8,128)(2,1)S(1)}, u32[]{:S(2)}, u32[]{:S(2)}) %collective-permute-start.3) | collective-permute-done | bytes 262176 | tf_op jit(solution)/shard_map/ppermute | solution.py:146
  48.5 0.1 add_convert_fusion
  48.6 0.7 %slice_bitcast_fusion = (bf16[1,1,256,256]{3,2,1,0:T(8,128)(2,1)}, bf16[1,1,256,256]{3,2,1,0:T(8,128)(2,1)}) fusion(bf16[512,256]{1,0:T(8,128)(2,1)S(1)} %add_convert_fusion), kind=kLoop, calls=%fused_computation.1 | loop fusion | bytes 524288 | tf_op jit(solution)/shard_map/broadcast_in_dim | solution.py:178
  (1 shorter events, 0.0 us)
Async XLA Ops:
  2.4 11.9 %collective-permute-start.2 = (bf16[512,256]{1,0:T(8,128)(2,1)}, bf16[512,256]{1,0:T(8,128)(2,1)S(1)}, u32[]{:S(2)}, u32[]{:S(2)}) collective-permute-start(bf16[512,256]{1,0:T(8,128)(2,1)} %pack.1.own_ref), channel_id=1, source_target_pairs={{0,16},{16,32},{32,48},{48,64},{64,80},{80,96},{96,112},{112,128},... | collective-permute-start | bytes 786440 | tf_op jit(solution)/shard_map/ppermute | solution.py:143
  7.0 17.3 %collective-permute-start.1 = (bf16[512,256]{1,0:T(8,128)(2,1)}, bf16[512,256]{1,0:T(8,128)(2,1)S(1)}, u32[]{:S(2)}, u32[]{:S(2)}) collective-permute-start(bf16[512,256]{1,0:T(8,128)(2,1)} %pack.1.own_ref), channel_id=1, source_target_pairs={{0,272},{16,288},{32,304},{48,320},{64,336},{80,352},{96,368},{112... | collective-permute-start | bytes 786440 | tf_op jit(solution)/shard_map/ppermute | solution.py:157
  10.3 14.0 %collective-permute-start = (bf16[512,256]{1,0:T(8,128)(2,1)}, bf16[512,256]{1,0:T(8,128)(2,1)S(1)}, u32[]{:S(2)}, u32[]{:S(2)}) collective-permute-start(bf16[512,256]{1,0:T(8,128)(2,1)} %pack.1.own_ref), channel_id=1, source_target_pairs={{0,256},{256,0},{1,257},{257,1},{2,258},{258,2},{3,259},{259,3},{4... | collective-permute-start | bytes 786440 | tf_op jit(solution)/shard_map/ppermute | solution.py:149
  14.3 1.0 %copy-start = (bf16[512,256]{1,0:T(8,128)(2,1)S(1)}, bf16[512,256]{1,0:T(8,128)(2,1)}, u32[]{:S(2)}) copy-start(bf16[512,256]{1,0:T(8,128)(2,1)} %pack.1.own_ref) | copy-start | bytes 786436
  15.2 1.2 %copy-start.1 = (bf16[1,1,128,4096]{3,2,1,0:T(8,128)(2,1)S(1)}, bf16[1,1,128,4096]{3,2,1,0:T(8,128)(2,1)}, u32[]{:S(2)}) copy-start(bf16[1,1,128,4096]{3,2,1,0:T(8,128)(2,1)} %param.7) | copy-start | bytes 3145732
  16.4 1.2 %copy-start.2 = (bf16[1,1,128,4096]{3,2,1,0:T(8,128)(2,1)S(1)}, bf16[1,1,128,4096]{3,2,1,0:T(8,128)(2,1)}, u32[]{:S(2)}) copy-start(bf16[1,1,128,4096]{3,2,1,0:T(8,128)(2,1)} %param.8) | copy-start | bytes 3145732
  30.9 10.2 %collective-permute-start.4 = (bf16[512,256]{1,0:T(8,128)(2,1)S(1)}, bf16[512,256]{1,0:T(8,128)(2,1)S(1)}, u32[]{:S(2)}, u32[]{:S(2)}) collective-permute-start(bf16[512,256]{1,0:T(8,128)(2,1)S(1)} %get-tuple-element.13), channel_id=1, source_target_pairs={{0,256},{256,0},{1,257},{257,1},{2,258},{258,2},{3,259},{259,3},{4... | collective-permute-start | bytes 786440 | tf_op jit(solution)/shard_map/ppermute | solution.py:149
  34.6 13.3 %collective-permute-start.5 = (bf16[512,256]{1,0:T(8,128)(2,1)S(1)}, bf16[512,256]{1,0:T(8,128)(2,1)S(1)}, u32[]{:S(2)}, u32[]{:S(2)}) collective-permute-start(bf16[512,256]{1,0:T(8,128)(2,1)S(1)} %get-tuple-element.14), channel_id=1, source_target_pairs={{16,256},{32,272},{48,288},{64,304},{80,320},{96,336},{112,352},{1... | collective-permute-start | bytes 786440 | tf_op jit(solution)/shard_map/ppermute | solution.py:157
  38.9 9.6 %collective-permute-start.3 = (bf16[512,256]{1,0:T(8,128)(2,1)S(1)}, bf16[512,256]{1,0:T(8,128)(2,1)S(1)}, u32[]{:S(2)}, u32[]{:S(2)}) collective-permute-start(bf16[512,256]{1,0:T(8,128)(2,1)S(1)} %get-tuple-element.12), channel_id=1, source_target_pairs={{16,0},{32,16},{48,32},{64,48},{80,64},{96,80},{112,96},{128,112},... | collective-permute-start | bytes 786440 | tf_op jit(solution)/shard_map/ppermute | solution.py:146

commit v2 on v1

v2 whole, which is shorter than its diff:
```python
import functools

import jax
import jax.numpy as jnp
from jax import lax
from jax.experimental import pallas as pl
from jax.experimental.pallas import tpu as pltpu
from jax.sharding import PartitionSpec as P

QUERY_HEADS = 32
KEY_VALUE_HEADS = 4
HEAD_SIZE = 128
ROWS_PER_SCALE = 128
GROUP = QUERY_HEADS // KEY_VALUE_HEADS
FACTOR = HEAD_SIZE**-0.5
LOG2_E = 1.4426950408889634
NEG_FILL = -1e30
PAIR = 8


def nt(a, b):
    return lax.dot_general(a, b, (((1,), (1,)), ((), ())), preferred_element_type=jnp.float32)


def nn(a, b):
    return lax.dot_general(a, b, (((1,), (0,)), ((), ())), preferred_element_type=jnp.float32)


def in_vmem(shape, dtype):
    return pltpu.VMEM(shape, dtype)


def pinned(value, space):
    return pltpu.with_memory_space_constraint(value, space)


def pack_kernel(
    key_exps, value_exps, reach, key_hbm, value_hbm, q_hbm, g_hbm,
    out_ref, bias_ref, q_ref, g_ref, key_ref, value_ref, sem,
):
    pairs = ((key_hbm, key_ref), (value_hbm, value_ref), (q_hbm, q_ref), (g_hbm, g_ref))
    loads = [pltpu.make_async_copy(*pair, sem.at[at]) for at, pair in enumerate(pairs)]
    for load in loads:
        load.start()
    length = key_ref.shape[0]
    tokens = q_ref.shape[0]
    rows = lax.broadcasted_iota(jnp.int32, (2 * length, tokens), 0)
    cols = lax.broadcasted_iota(jnp.int32, (2 * length, tokens), 1)
    last = jnp.where(rows < length, length, cols + (length + lax.axis_index("head") * tokens))
    lowest = jnp.where(lax.axis_index("inner") == 0, length, length - reach[0, 0])
    visible = jnp.logical_and(rows >= lowest, rows <= last)
    bias_ref[...] = jnp.where(visible, 0.0, NEG_FILL).astype(jnp.bfloat16)
    for load, source, exps, base in (
        (loads[0], key_ref, key_exps, 0),
        (loads[1], value_ref, value_exps, length),
    ):
        load.wait()
        for run in range(length // ROWS_PER_SCALE):
            part = slice(run * ROWS_PER_SCALE, (run + 1) * ROWS_PER_SCALE)
            to = slice(base + part.start, base + part.stop)
            for head in range(source.shape[1] // HEAD_SIZE):
                at = slice(head * HEAD_SIZE, (head + 1) * HEAD_SIZE)
                exponent = jnp.full((8, HEAD_SIZE), exps[run, head], jnp.int32).astype(jnp.float32)
                scale = jnp.exp2(exponent)[:1].astype(jnp.bfloat16)
                out_ref[to, at] = source[part, at] * scale
    for load in loads[2:]:
        load.wait()


def pack(key_mant, value_mant, key_exps, value_exps, reach, query, dout):
    length, width = key_mant.shape
    tokens = query.shape[0]
    smem = pl.BlockSpec(memory_space=pltpu.SMEM)
    vmem = pl.BlockSpec(memory_space=pltpu.VMEM)
    hbm = pl.BlockSpec(memory_space=pltpu.HBM)
    return pl.pallas_call(
        pack_kernel,
        out_shape=(
            in_vmem((2 * length, width), jnp.bfloat16),
            in_vmem((2 * length, tokens), jnp.bfloat16),
            in_vmem(query.shape, jnp.bfloat16),
            in_vmem(dout.shape, jnp.bfloat16),
        ),
        in_specs=[smem] * 3 + [hbm] * 4,
        out_specs=[vmem] * 4,
        scratch_shapes=[
            pltpu.VMEM((length, width), jnp.bfloat16),
            pltpu.VMEM((length, width), jnp.bfloat16),
            pltpu.SemaphoreType.DMA((4,)),
        ],
        compiler_params=pltpu.CompilerParams(vmem_limit_bytes=16 * 1024 * 1024),
        name="pack",
    )(key_exps, value_exps, reach, *(pinned(x, pltpu.HBM) for x in (key_mant, value_mant, query, dout)))


def attend_kernel(remote, bias_ref, q_ref, g_ref, own_ref, prev_ref, *refs):
    dq_hbm, next_ref, term_ref, dq_ref, sem = refs[-5:]
    tokens = q_ref.shape[0]
    length = own_ref.shape[0] // 2
    heads = own_ref.shape[1] // HEAD_SIZE
    wide = GROUP * HEAD_SIZE
    span = PAIR * HEAD_SIZE
    group = lax.axis_index("head")
    base = (1 - group if remote else group) * (heads * wide)
    bias = bias_ref[...]
    ident = (
        lax.broadcasted_iota(jnp.int32, (tokens, tokens), 0)
        == lax.broadcasted_iota(jnp.int32, (tokens, tokens), 1)
    )
    ident = jnp.where(ident, 1.0, 0.0).astype(jnp.bfloat16)
    ident = jnp.concatenate([ident] * PAIR, axis=0)

    def column(head):
        return pl.ds(pl.multiple_of(base + head * HEAD_SIZE, HEAD_SIZE), HEAD_SIZE)

    def stacked(ref, step):
        return jnp.concatenate(
            [ref[:, column(h)] for h in range(step * PAIR, (step + 1) * PAIR)], axis=0
        )

    def keys_of(kv):
        at = slice(kv * HEAD_SIZE, (kv + 1) * HEAD_SIZE)
        return jnp.concatenate([prev_ref[:length, at], own_ref[:length, at]], axis=0)

    def values_of(kv):
        at = slice(kv * HEAD_SIZE, (kv + 1) * HEAD_SIZE)
        return jnp.concatenate([prev_ref[length:, at], own_ref[length:, at]], axis=0)

    def project(step):
        kv = step * PAIR // GROUP
        masked_keys = jnp.concatenate([keys_of(kv), bias], axis=1)
        scores = nt(masked_keys, jnp.concatenate([stacked(q_ref, step), ident], axis=1))
        return scores, nt(values_of(kv), stacked(g_ref, step))

    def soften(scores, dprob):
        peak = jnp.max(scores, axis=0, keepdims=True)
        weights = jnp.exp2((scores - peak) * (FACTOR * LOG2_E))
        inverse = 1.0 / jnp.sum(weights, axis=0, keepdims=True)
        row_dot = jnp.sum(weights * dprob, axis=0, keepdims=True) * inverse
        probs = weights * inverse
        dscore = (probs * (dprob - row_dot)).astype(jnp.bfloat16)
        return probs.astype(jnp.bfloat16), dscore

    def finish(step, dscore):
        kv = step * PAIR // GROUP
        dq = (nn(keys_of(kv).T, dscore) * FACTOR).astype(jnp.bfloat16).T
        for i in range(PAIR):
            h = step * PAIR + i
            dq_ref[:, h * HEAD_SIZE : (h + 1) * HEAD_SIZE] = dq[i * tokens : (i + 1) * tokens]

    def send(kv):
        at = slice(kv * wide, (kv + 1) * wide)
        to = pl.ds(pl.multiple_of(base + kv * wide, HEAD_SIZE), wide)
        return pltpu.make_async_copy(dq_ref.at[:, at], dq_hbm.at[:, to], sem.at[kv])

    def gather(step, probs, dscore):
        return nn(dscore, stacked(q_ref, step)), nn(probs, stacked(g_ref, step))

    def deliver(kv, dk, dv):
        dk = dk * FACTOR
        at = slice(kv * HEAD_SIZE, (kv + 1) * HEAD_SIZE)
        next_ref[:length, at] = dk[:length].astype(next_ref.dtype)
        next_ref[length:, at] = dv[:length].astype(next_ref.dtype)
        term_ref[:length, at] = dk[length:].astype(term_ref.dtype)
        term_ref[length:, at] = dv[length:].astype(term_ref.dtype)

    steps = heads * GROUP // PAIR
    per = GROUP // PAIR
    raw = project(0)
    sums = [[0.0, 0.0] for _ in range(heads)]
    for step in range(steps):
        ahead = project(step + 1) if step + 1 < steps else None
        probs, dscore = soften(*raw)
        raw = ahead
        finish(step, dscore)
        kv = step // per
        parts = gather(step, probs, dscore)
        sums[kv] = [x + y for x, y in zip(sums[kv], parts)]
        if (step + 1) % per == 0:
            send(kv).start()
            deliver(kv, *sums[kv])
    for kv in range(heads):
        send(kv).wait()


def attend(remote, bias, query, dout, own, prev, dq_so_far, term_dtype, name):
    tokens, width = query.shape
    rows, half = own.shape
    heads = half // HEAD_SIZE
    vmem = pl.BlockSpec(memory_space=pltpu.VMEM)
    operands = [pinned(x, pltpu.VMEM) for x in (bias, query, dout, own, prev)]
    in_specs = [vmem] * 5
    aliases = {}
    if dq_so_far is not None:
        operands.append(dq_so_far)
        in_specs.append(pl.BlockSpec(memory_space=pl.ANY))
        aliases = {5: 0}
    lanes = heads * GROUP * HEAD_SIZE
    return pl.pallas_call(
        functools.partial(attend_kernel, remote),
        out_shape=(
            jax.ShapeDtypeStruct((tokens, width), jnp.bfloat16),
            in_vmem((rows, half), jnp.bfloat16),
            in_vmem((rows, half), term_dtype),
        ),
        in_specs=in_specs,
        out_specs=[pl.BlockSpec(memory_space=pl.ANY), vmem, vmem],
        scratch_shapes=[pltpu.VMEM((tokens, lanes), jnp.bfloat16), pltpu.SemaphoreType.DMA((heads,))],
        input_output_aliases=aliases,
        cost_estimate=pl.CostEstimate(
            flops=10 * heads * GROUP * tokens * rows * HEAD_SIZE,
            bytes_accessed=4 * 1024 * 1024,
            transcendentals=heads * GROUP * tokens * rows,
        ),
        compiler_params=pltpu.CompilerParams(vmem_limit_bytes=32 * 1024 * 1024),
        name=name,
    )(*operands)


def on_device(query, dout, key_mant, value_mantissas, key_exps, value_exponents, reach):
    inner = lax.axis_size("inner")
    length = key_mant.shape[2]
    query_rows, dout_rows = query[0, 0], dout[0, 0]
    own, bias, query_rows, dout_rows = pack(
        key_mant[0, 0],
        value_mantissas[0, 0],
        key_exps[0, 0],
        value_exponents[0, 0],
        reach,
        query_rows,
        dout_rows,
    )

    def forward(value):
        return lax.ppermute(value, "inner", [(i, i + 1) for i in range(inner - 1)])

    def backward(value):
        return lax.ppermute(value, "inner", [(i + 1, i) for i in range(inner - 1)])

    def swap(value):
        return lax.ppermute(value, "head", [(0, 1), (1, 0)])

    def across(value, step):
        pairs = [
            (head * inner + at, (1 - head) * inner + at + step)
            for head in range(2)
            for at in range(max(0, -step), min(inner, inner - step))
        ]
        return lax.ppermute(value, ("head", "inner"), pairs)

    prev = forward(own)
    other_own = swap(own)
    other_prev = across(own, 1)
    dq, next_here, term_here = attend(
        False, bias, query_rows, dout_rows, own, prev, None, jnp.float32, "attend_local"
    )
    returned = backward(next_here)
    dq, next_there, term_there = attend(
        True, bias, query_rows, dout_rows, other_own, other_prev, dq, jnp.bfloat16, "attend_remote"
    )
    swapped = swap(term_there)
    crossed = across(next_there, -1)
    total = term_here
    for part in (returned, swapped, crossed):
        total = total + part.astype(jnp.float32)
    total = total.astype(jnp.bfloat16)
    return dq[None, None], total[None, None, :length], total[None, None, length:]


def solution(mesh):
    placed = (
        P("outer", "inner", "head", None),
        P("outer", "inner", "head", None),
        P("outer", "inner", None, "head"),
        P("outer", "inner", None, "head"),
        P("outer", "inner", None, "head"),
        P("outer", "inner", None, "head"),
        P("outer", "inner"),
    )
    return jax.shard_map(
        on_device,
        mesh=mesh,
        in_specs=placed,
        out_specs=(
            P("outer", "inner", "head", None),
            P("outer", "inner", None, "head"),
            P("outer", "inner", None, "head"),
        ),
        check_vma=False,
    )
```

time: 49.7 us -> 47.8 us (0.962)
  the two profiles are of different devices: /device:TPU:1 before, /device:TPU:7 now
where the time goes in v2:
time: 47.8 us; the launch traced here: 47.5 us
  starting transfers between devices  20.3 us (42%)
  waiting for transfers between devices  13.2 us (28%)
  Pallas kernels  11.1 us (23%)
  local copies, waits for them, and re-layouts  1.4 us (3%)
  between operations  1.39 us (3%)
    ppermute x2, waiting for transfers between devices, across(): return lax.ppermute(value, ('head', 'inner'), pairs)  11.1 us
    ppermute x2, starting transfers between devices, across(): return lax.ppermute(value, ('head', 'inner'), pairs)  9.59 us
    pallas_call x2, Pallas kernels, attend(): pl.pallas_call(functools.partial(attend_kernel, remote), out_shape=(jax.S...  8.82 us
    ppermute x2, starting transfers between devices, swap(): return lax.ppermute(value, 'head', [(0, 1), (1, 0)])  5.01 us
    ppermute x1, starting transfers between devices, forward(): return lax.ppermute(value, 'inner', [(i, i + 1) for i in range(inner - 1)])  3.77 us
    pallas_call x1, Pallas kernels, pack(): pl.pallas_call(pack_kernel, out_shape=(in_vmem((2 * length, width), jnp.b...  2.28 us
    ppermute x2, waiting for transfers between devices, swap(): return lax.ppermute(value, 'head', [(0, 1), (1, 0)])  2.05 us
    ppermute x1, starting transfers between devices, backward(): return lax.ppermute(value, 'inner', [(i + 1, i) for i in range(inner - 1)])  1.92 us
  transfers between devices with their start and end apart: 6, of which 3 were waited for; matrix products, arithmetic and copies ran while one was open for 0% of the time, Pallas kernels for 9%

profile of v2, /device:TPU:7, one launch (start us, length us, event | category | flops | bytes accessed | tf_op | source)
XLA Modules:
  0.0 47.5 jit_solution(4136418777931510092)
XLA Ops:
  1.3 0.0 copy-start.1
  1.3 0.0 copy-start
  1.3 0.7 %copy-done.1 = s32[1,1,2,2]{3,2,1,0:T(2,128)S(1)} copy-done((s32[1,1,2,2]{3,2,1,0:T(2,128)S(1)}, s32[1,1,2,2]{3,2,1,0:T(2,128)}, u32[]{:S(2)}) %copy-start.1) | copy-done | bytes 40
  2.0 0.0 copy-done
  2.0 2.3 %pack.1 = (bf16[512,256]{1,0:T(8,128)(2,1)S(1)}, bf16[512,128]{1,0:T(8,128)(2,1)S(1)}, bf16[128,4096]{1,0:T(8,128)(2,1)S(1)}, bf16[128,4096]{1,0:T(8,128)(2,1)S(1)}) custom-call(s32[2,2]{1,0:T(2,128)S(1)} %bitcast.11, s32[2,2]{1,0:T(2,128)S(1)} %bitcast.12, s32[1,1]{1,0:T(1,128)S(6)} %copy.12.reach, bf16[256,256]{1,0:T(8,128)(2,1)} %bitcast.15, ...), custom_call_target="tpu_custom_call" | custom-call | tf_op jit(solution)/shard_map/pack/pallas_call | solution.py:76
  4.3 3.8 %collective-permute-start.2 = (bf16[512,256]{1,0:T(8,128)(2,1)S(1)}, bf16[512,256]{1,0:T(8,128)(2,1)S(1)}, u32[]{:S(2)}, u32[]{:S(2)}) collective-permute-start(bf16[512,256]{1,0:T(8,128)(2,1)S(1)} %get-tuple-element.16.own_ref), channel_id=1, source_target_pairs={{0,16},{16,32},{32,48},{48,64},{64,80},{80,96},{96,112},{112,128},... | collective-permute-start | bytes 786440 | tf_op jit(solution)/shard_map/ppermute | solution.py:235
  8.0 3.4 %collective-permute-start.1 = (bf16[512,256]{1,0:T(8,128)(2,1)S(1)}, bf16[512,256]{1,0:T(8,128)(2,1)S(1)}, u32[]{:S(2)}, u32[]{:S(2)}) collective-permute-start(bf16[512,256]{1,0:T(8,128)(2,1)S(1)} %get-tuple-element.16.own_ref), channel_id=1, source_target_pairs={{0,272},{16,288},{32,304},{48,320},{64,336},{80,352},{96,368},{112... | collective-permute-start | bytes 786440 | tf_op jit(solution)/shard_map/ppermute | solution.py:249
  11.4 3.1 %collective-permute-start = (bf16[512,256]{1,0:T(8,128)(2,1)S(1)}, bf16[512,256]{1,0:T(8,128)(2,1)S(1)}, u32[]{:S(2)}, u32[]{:S(2)}) collective-permute-start(bf16[512,256]{1,0:T(8,128)(2,1)S(1)} %get-tuple-element.16.own_ref), channel_id=1, source_target_pairs={{0,256},{256,0},{1,257},{257,1},{2,258},{258,2},{3,259},{259,3},{4... | collective-permute-start | bytes 786440 | tf_op jit(solution)/shard_map/ppermute | solution.py:241
  14.5 0.0 collective-permute-done.2.prev_ref
  14.5 4.4 %attend_local.1 = (bf16[128,4096]{1,0:T(8,128)(2,1)}, bf16[512,256]{1,0:T(8,128)(2,1)S(1)}, f32[512,256]{1,0:T(8,128)S(1)}) custom-call(bf16[512,128]{1,0:T(8,128)(2,1)S(1)} %get-tuple-element.13.bias_ref, bf16[128,4096]{1,0:T(8,128)(2,1)S(1)} %get-tuple-element.14.q_ref, bf16[128,4096]{1,0:T(8,128)(2,1)S(1)} %get-tuple-element.15.g_ref, ...), custom_call_target="tpu_custom_call" | custom-call | flops 1342177280 | bytes 4194304 | tf_op jit(solution)/shard_map/attend_local/pallas_call | solution.py:199
  18.9 4.2 %collective-permute-done.1.prev_ref = bf16[512,256]{1,0:T(8,128)(2,1)S(1)} collective-permute-done((bf16[512,256]{1,0:T(8,128)(2,1)S(1)}, bf16[512,256]{1,0:T(8,128)(2,1)S(1)}, u32[]{:S(2)}, u32[]{:S(2)}) %collective-permute-start.1) | collective-permute-done | bytes 262176 | tf_op jit(solution)/shard_map/ppermute | solution.py:249
  23.1 2.0 %collective-permute-done.own_ref = bf16[512,256]{1,0:T(8,128)(2,1)S(1)} collective-permute-done((bf16[512,256]{1,0:T(8,128)(2,1)S(1)}, bf16[512,256]{1,0:T(8,128)(2,1)S(1)}, u32[]{:S(2)}, u32[]{:S(2)}) %collective-permute-start) | collective-permute-done | bytes 262176 | tf_op jit(solution)/shard_map/ppermute | solution.py:241
  25.1 4.4 %attend_remote.1 = (bf16[128,4096]{1,0:T(8,128)(2,1)}, bf16[512,256]{1,0:T(8,128)(2,1)S(1)}, bf16[512,256]{1,0:T(8,128)(2,1)S(1)}) custom-call(bf16[512,128]{1,0:T(8,128)(2,1)S(1)} %get-tuple-element.13.bias_ref, bf16[128,4096]{1,0:T(8,128)(2,1)S(1)} %get-tuple-element.14.q_ref, ...), custom_call_target="tpu_custom_call", output_to_operand_aliasing={{0}: (5, {})} | custom-call | flops 1342177280 | bytes 4194304 | tf_op jit(solution)/shard_map/attend_remote/pallas_call | solution.py:199
  29.6 1.9 %collective-permute-start.4 = (bf16[512,256]{1,0:T(8,128)(2,1)S(1)}, bf16[512,256]{1,0:T(8,128)(2,1)S(1)}, u32[]{:S(2)}, u32[]{:S(2)}) collective-permute-start(bf16[512,256]{1,0:T(8,128)(2,1)S(1)} %get-tuple-element.21), channel_id=1, source_target_pairs={{0,256},{256,0},{1,257},{257,1},{2,258},{258,2},{3,259},{259,3},{4... | collective-permute-start | bytes 786440 | tf_op jit(solution)/shard_map/ppermute | solution.py:241
  31.5 6.2 %collective-permute-start.5 = (bf16[512,256]{1,0:T(8,128)(2,1)S(1)}, bf16[512,256]{1,0:T(8,128)(2,1)S(1)}, u32[]{:S(2)}, u32[]{:S(2)}) collective-permute-start(bf16[512,256]{1,0:T(8,128)(2,1)S(1)} %get-tuple-element.22), channel_id=1, source_target_pairs={{16,256},{32,272},{48,288},{64,304},{80,320},{96,336},{112,352},{1... | collective-permute-start | bytes 786440 | tf_op jit(solution)/shard_map/ppermute | solution.py:249
  37.7 1.9 %collective-permute-start.3 = (bf16[512,256]{1,0:T(8,128)(2,1)S(1)}, bf16[512,256]{1,0:T(8,128)(2,1)S(1)}, u32[]{:S(2)}, u32[]{:S(2)}) collective-permute-start(bf16[512,256]{1,0:T(8,128)(2,1)S(1)} %get-tuple-element.20), channel_id=1, source_target_pairs={{16,0},{32,16},{48,32},{64,48},{80,64},{96,80},{112,96},{128,112},... | collective-permute-start | bytes 786440 | tf_op jit(solution)/shard_map/ppermute | solution.py:238
  39.7 0.0 collective-permute-done.4
  39.7 6.9 %collective-permute-done.5 = bf16[512,256]{1,0:T(8,128)(2,1)S(1)} collective-permute-done((bf16[512,256]{1,0:T(8,128)(2,1)S(1)}, bf16[512,256]{1,0:T(8,128)(2,1)S(1)}, u32[]{:S(2)}, u32[]{:S(2)}) %collective-permute-start.5) | collective-permute-done | bytes 262176 | tf_op jit(solution)/shard_map/ppermute | solution.py:249
  46.6 0.0 collective-permute-done.3
  46.6 0.1 add_convert_fusion
  46.7 0.7 %slice_bitcast_fusion = (bf16[1,1,256,256]{3,2,1,0:T(8,128)(2,1)}, bf16[1,1,256,256]{3,2,1,0:T(8,128)(2,1)}) fusion(bf16[512,256]{1,0:T(8,128)(2,1)S(1)} %add_convert_fusion), kind=kLoop, calls=%fused_computation.1 | loop fusion | bytes 524288 | tf_op jit(solution)/shard_map/broadcast_in_dim | solution.py:267
Async XLA Ops:
  1.3 0.7 %copy-start.1 = (s32[1,1,2,2]{3,2,1,0:T(2,128)S(1)}, s32[1,1,2,2]{3,2,1,0:T(2,128)}, u32[]{:S(2)}) copy-start(s32[1,1,2,2]{3,2,1,0:T(2,128)} %param.12) | copy-start | bytes 52
  1.3 0.7 %copy-start = (s32[1,1,2,2]{3,2,1,0:T(2,128)S(1)}, s32[1,1,2,2]{3,2,1,0:T(2,128)}, u32[]{:S(2)}) copy-start(s32[1,1,2,2]{3,2,1,0:T(2,128)} %param.11) | copy-start | bytes 52
  4.3 10.2 %collective-permute-start.2 = (bf16[512,256]{1,0:T(8,128)(2,1)S(1)}, bf16[512,256]{1,0:T(8,128)(2,1)S(1)}, u32[]{:S(2)}, u32[]{:S(2)}) collective-permute-start(bf16[512,256]{1,0:T(8,128)(2,1)S(1)} %get-tuple-element.16.own_ref), channel_id=1, source_target_pairs={{0,16},{16,32},{32,48},{48,64},{64,80},{80,96},{96,112},{112,128},... | collective-permute-start | bytes 786440 | tf_op jit(solution)/shard_map/ppermute | solution.py:235
  8.0 15.1 %collective-permute-start.1 = (bf16[512,256]{1,0:T(8,128)(2,1)S(1)}, bf16[512,256]{1,0:T(8,128)(2,1)S(1)}, u32[]{:S(2)}, u32[]{:S(2)}) collective-permute-start(bf16[512,256]{1,0:T(8,128)(2,1)S(1)} %get-tuple-element.16.own_ref), channel_id=1, source_target_pairs={{0,272},{16,288},{32,304},{48,320},{64,336},{80,352},{96,368},{112... | collective-permute-start | bytes 786440 | tf_op jit(solution)/shard_map/ppermute | solution.py:249
  11.4 13.7 %collective-permute-start = (bf16[512,256]{1,0:T(8,128)(2,1)S(1)}, bf16[512,256]{1,0:T(8,128)(2,1)S(1)}, u32[]{:S(2)}, u32[]{:S(2)}) collective-permute-start(bf16[512,256]{1,0:T(8,128)(2,1)S(1)} %get-tuple-element.16.own_ref), channel_id=1, source_target_pairs={{0,256},{256,0},{1,257},{257,1},{2,258},{258,2},{3,259},{259,3},{4... | collective-permute-start | bytes 786440 | tf_op jit(solution)/shard_map/ppermute | solution.py:241
  29.6 10.1 %collective-permute-start.4 = (bf16[512,256]{1,0:T(8,128)(2,1)S(1)}, bf16[512,256]{1,0:T(8,128)(2,1)S(1)}, u32[]{:S(2)}, u32[]{:S(2)}) collective-permute-start(bf16[512,256]{1,0:T(8,128)(2,1)S(1)} %get-tuple-element.21), channel_id=1, source_target_pairs={{0,256},{256,0},{1,257},{257,1},{2,258},{258,2},{3,259},{259,3},{4... | collective-permute-start | bytes 786440 | tf_op jit(solution)/shard_map/ppermute | solution.py:241
  31.5 15.1 %collective-permute-start.5 = (bf16[512,256]{1,0:T(8,128)(2,1)S(1)}, bf16[512,256]{1,0:T(8,128)(2,1)S(1)}, u32[]{:S(2)}, u32[]{:S(2)}) collective-permute-start(bf16[512,256]{1,0:T(8,128)(2,1)S(1)} %get-tuple-element.22), channel_id=1, source_target_pairs={{16,256},{32,272},{48,288},{64,304},{80,320},{96,336},{112,352},{1... | collective-permute-start | bytes 786440 | tf_op jit(solution)/shard_map/ppermute | solution.py:249
  37.7 8.9 %collective-permute-start.3 = (bf16[512,256]{1,0:T(8,128)(2,1)S(1)}, bf16[512,256]{1,0:T(8,128)(2,1)S(1)}, u32[]{:S(2)}, u32[]{:S(2)}) collective-permute-start(bf16[512,256]{1,0:T(8,128)(2,1)S(1)} %get-tuple-element.20), channel_id=1, source_target_pairs={{16,0},{32,16},{48,32},{64,48},{80,64},{96,80},{112,96},{128,112},... | collective-permute-start | bytes 786440 | tf_op jit(solution)/shard_map/ppermute | solution.py:238

commit v3 on v2

--- a/solution.py
+++ b/solution.py
@@ -16,6 +16,8 @@
 LOG2_E = 1.4426950408889634
 NEG_FILL = -1e30
 PAIR = 8
+PACK_FLOPS = 8 * 10**9
+PACK_VMEM = 48
 
 
 def nt(a, b):
@@ -35,21 +37,19 @@
 
 
 def pack_kernel(
-    key_exps, value_exps, reach, key_hbm, value_hbm, q_hbm, g_hbm,
-    out_ref, bias_ref, q_ref, g_ref, key_ref, value_ref, sem,
+    key_exps_hbm, value_exps_hbm, key_hbm, value_hbm, out_ref, key_ref, value_ref, key_exps, value_exps, sem
 ):
-    pairs = ((key_hbm, key_ref), (value_hbm, value_ref), (q_hbm, q_ref), (g_hbm, g_ref))
-    loads = [pltpu.make_async_copy(*pair, sem.at[at]) for at, pair in enumerate(pairs)]
+    length = key_ref.shape[0]
+    loads = [
+        pltpu.make_async_copy(key_hbm, key_ref, sem.at[0]),
+        pltpu.make_async_copy(value_hbm, value_ref, sem.at[1]),
+        pltpu.make_async_copy(key_exps_hbm, key_exps, sem.at[2]),
+        pltpu.make_async_copy(value_exps_hbm, value_exps, sem.at[3]),
+    ]
     for load in loads:
         load.start()
-    length = key_ref.shape[0]
-    tokens = q_ref.shape[0]
-    rows = lax.broadcasted_iota(jnp.int32, (2 * length, tokens), 0)
-    cols = lax.broadcasted_iota(jnp.int32, (2 * length, tokens), 1)
-    last = jnp.where(rows < length, length, cols + (length + lax.axis_index("head") * tokens))
-    lowest = jnp.where(lax.axis_index("inner") == 0, length, length - reach[0, 0])
-    visible = jnp.logical_and(rows >= lowest, rows <= last)
-    bias_ref[...] = jnp.where(visible, 0.0, NEG_FILL).astype(jnp.bfloat16)
+    for load in loads[2:]:
+        load.wait()
     for load, source, exps, base in (
         (loads[0], key_ref, key_exps, 0),
         (loads[1], value_ref, value_exps, length),
@@ -63,38 +63,52 @@
                 exponent = jnp.full((8, HEAD_SIZE), exps[run, head], jnp.int32).astype(jnp.float32)
                 scale = jnp.exp2(exponent)[:1].astype(jnp.bfloat16)
                 out_ref[to, at] = source[part, at] * scale
-    for load in loads[2:]:
-        load.wait()
-
-
-def pack(key_mant, value_mant, key_exps, value_exps, reach, query, dout):
+
+
+def pack(key_mant, value_mant, key_exps, value_exps):
     length, width = key_mant.shape
-    tokens = query.shape[0]
-    smem = pl.BlockSpec(memory_space=pltpu.SMEM)
     vmem = pl.BlockSpec(memory_space=pltpu.VMEM)
     hbm = pl.BlockSpec(memory_space=pltpu.HBM)
     return pl.pallas_call(
         pack_kernel,
-        out_shape=(
-            in_vmem((2 * length, width), jnp.bfloat16),
-            in_vmem((2 * length, tokens), jnp.bfloat16),
-            in_vmem(query.shape, jnp.bfloat16),
-            in_vmem(dout.shape, jnp.bfloat16),
-        ),
-        in_specs=[smem] * 3 + [hbm] * 4,
-        out_specs=[vmem] * 4,
+        out_shape=in_vmem((2 * length, width), jnp.bfloat16),
+        in_specs=[hbm] * 4,
+        out_specs=vmem,
         scratch_shapes=[
             pltpu.VMEM((length, width), jnp.bfloat16),
             pltpu.VMEM((length, width), jnp.bfloat16),
+            pltpu.SMEM(key_exps.shape, jnp.int32),
+            pltpu.SMEM(value_exps.shape, jnp.int32),
             pltpu.SemaphoreType.DMA((4,)),
         ],
-        compiler_params=pltpu.CompilerParams(vmem_limit_bytes=16 * 1024 * 1024),
+        cost_estimate=pl.CostEstimate(flops=PACK_FLOPS, bytes_accessed=1024 * 1024, transcendentals=0),
+        compiler_params=pltpu.CompilerParams(vmem_limit_bytes=PACK_VMEM * 1024 * 1024),
         name="pack",
-    )(key_exps, value_exps, reach, *(pinned(x, pltpu.HBM) for x in (key_mant, value_mant, query, dout)))
-
-
-def attend_kernel(remote, bias_ref, q_ref, g_ref, own_ref, prev_ref, *refs):
-    dq_hbm, next_ref, term_ref, dq_ref, sem = refs[-5:]
+    )(*(pinned(x, pltpu.HBM) for x in (key_exps, value_exps, key_mant, value_mant)))
+
+
+def fetch(reach_hbm, reach_ref, bias_ref, q_ref, sem):
+    group = lax.axis_index("head")
+    bound = pltpu.make_async_copy(reach_hbm, reach_ref, sem.at[0])
+    bound.start()
+    tokens = q_ref.shape[0]
+    length = bias_ref.shape[0] // 2
+    rows = lax.broadcasted_iota(jnp.int32, bias_ref.shape, 0)
+    cols = lax.broadcasted_iota(jnp.int32, bias_ref.shape, 1)
+    last = jnp.where(rows < length, length, cols + (length + group * tokens))
+    bound.wait()
+    lowest = jnp.where(lax.axis_index("inner") == 0, length, length - reach_ref[...])
+    visible = jnp.logical_and(rows >= lowest, rows <= last)
+    bias_ref[...] = jnp.where(visible, 0.0, NEG_FILL).astype(jnp.bfloat16)
+
+
+def attend_kernel(remote, *refs):
+    if remote:
+        bias_ref, q_ref, g_ref, own_ref, prev_ref, _, dq_hbm, next_ref, term_ref, dq_ref, sem = refs
+    else:
+        reach_hbm, q_ref, g_ref, own_ref, prev_ref, _ = refs[:6]
+        dq_hbm, next_ref, term_ref, bias_ref, dq_ref, sem, load_sem, reach_ref = refs[6:]
+        fetch(reach_hbm, reach_ref, bias_ref, q_ref, load_sem)
     tokens = q_ref.shape[0]
     length = own_ref.shape[0] // 2
     heads = own_ref.shape[1] // HEAD_SIZE
@@ -183,30 +197,45 @@
         send(kv).wait()
 
 
-def attend(remote, bias, query, dout, own, prev, dq_so_far, term_dtype, name):
-    tokens, width = query.shape
+def attend(own, prev, loads, held, ready, name):
+    remote = held is not None
     rows, half = own.shape
     heads = half // HEAD_SIZE
     vmem = pl.BlockSpec(memory_space=pltpu.VMEM)
-    operands = [pinned(x, pltpu.VMEM) for x in (bias, query, dout, own, prev)]
-    in_specs = [vmem] * 5
-    aliases = {}
-    if dq_so_far is not None:
-        operands.append(dq_so_far)
-        in_specs.append(pl.BlockSpec(memory_space=pl.ANY))
-        aliases = {5: 0}
+    anywhere = pl.BlockSpec(memory_space=pl.ANY)
     lanes = heads * GROUP * HEAD_SIZE
+    kept = [pinned(x, pltpu.VMEM) for x in (own, prev)]
+    if remote:
+        dq, bias, query, dout = held
+        tokens, width = query.shape
+        operands = [pinned(x, pltpu.VMEM) for x in (bias, query, dout)] + kept + [dq]
+        in_specs = [vmem] * 5 + [anywhere]
+        more_shapes, more_specs, more_scratch = (), [], []
+    else:
+        tokens, width = loads[1].shape
+        operands = [loads[0]] + [pinned(x, pltpu.VMEM) for x in loads[1:]] + kept + [ready]
+        in_specs = [anywhere] + [vmem] * 4 + [anywhere]
+        more_shapes = (
+            in_vmem((rows, tokens), jnp.bfloat16),
+        )
+        more_specs = [vmem]
+        more_scratch = [pltpu.SemaphoreType.DMA((1,)), pltpu.VMEM((1, 1), jnp.int32)]
     return pl.pallas_call(
         functools.partial(attend_kernel, remote),
         out_shape=(
             jax.ShapeDtypeStruct((tokens, width), jnp.bfloat16),
             in_vmem((rows, half), jnp.bfloat16),
-            in_vmem((rows, half), term_dtype),
-        ),
+            in_vmem((rows, half), jnp.bfloat16 if remote else jnp.float32),
+        )
+        + more_shapes,
         in_specs=in_specs,
-        out_specs=[pl.BlockSpec(memory_space=pl.ANY), vmem, vmem],
-        scratch_shapes=[pltpu.VMEM((tokens, lanes), jnp.bfloat16), pltpu.SemaphoreType.DMA((heads,))],
-        input_output_aliases=aliases,
+        out_specs=[anywhere, vmem, vmem] + more_specs,
+        scratch_shapes=[
+            pltpu.VMEM((tokens, lanes), jnp.bfloat16),
+            pltpu.SemaphoreType.DMA((heads,)),
+        ]
+        + more_scratch,
+        input_output_aliases={5: 0} if remote else {},
         cost_estimate=pl.CostEstimate(
             flops=10 * heads * GROUP * tokens * rows * HEAD_SIZE,
             bytes_accessed=4 * 1024 * 1024,
@@ -220,16 +249,7 @@
 def on_device(query, dout, key_mant, value_mantissas, key_exps, value_exponents, reach):
     inner = lax.axis_size("inner")
     length = key_mant.shape[2]
-    query_rows, dout_rows = query[0, 0], dout[0, 0]
-    own, bias, query_rows, dout_rows = pack(
-        key_mant[0, 0],
-        value_mantissas[0, 0],
-        key_exps[0, 0],
-        value_exponents[0, 0],
-        reach,
-        query_rows,
-        dout_rows,
-    )
+    own = pack(key_mant[0, 0], value_mantissas[0, 0], key_exps[0, 0], value_exponents[0, 0])
 
     def forward(value):
         return lax.ppermute(value, "inner", [(i, i + 1) for i in range(inner - 1)])
@@ -251,12 +271,13 @@
     prev = forward(own)
     other_own = swap(own)
     other_prev = across(own, 1)
-    dq, next_here, term_here = attend(
-        False, bias, query_rows, dout_rows, own, prev, None, jnp.float32, "attend_local"
+    loads = (reach, pinned(query[0, 0], pltpu.VMEM), pinned(dout[0, 0], pltpu.VMEM))
+    dq, next_here, term_here, *held = attend(
+        own, prev, loads, None, other_own, "attend_local"
     )
     returned = backward(next_here)
     dq, next_there, term_there = attend(
-        True, bias, query_rows, dout_rows, other_own, other_prev, dq, jnp.bfloat16, "attend_remote"
+        other_own, other_prev, None, (dq, *held, *loads[1:]), None, "attend_remote"
     )
     swapped = swap(term_there)
     crossed = across(next_there, -1)

time: 47.8 us -> 44.5 us (0.931)
  the two profiles are of different devices: /device:TPU:7 before, /device:TPU:1 now
where the time goes in v3:
time: 44.5 us; the launch traced here: 44.1 us
  starting transfers between devices  22.4 us (50%)
  Pallas kernels  10.1 us (23%)
  waiting for transfers between devices  9.44 us (21%)
  between operations  1.39 us (3%)
  local copies, waits for them, and re-layouts  0.72 us (2%)
    ppermute x2, starting transfers between devices, swap(): return lax.ppermute(value, 'head', [(0, 1), (1, 0)])  8.98 us
    pallas_call x2, Pallas kernels, attend(): pl.pallas_call(functools.partial(attend_kernel, remote), out_shape=(jax.S...  8.91 us
    ppermute x2, starting transfers between devices, across(): return lax.ppermute(value, ('head', 'inner'), pairs)  8.33 us
    ppermute x2, waiting for transfers between devices, across(): return lax.ppermute(value, ('head', 'inner'), pairs)  6.26 us
    ppermute x1, starting transfers between devices, forward(): return lax.ppermute(value, 'inner', [(i, i + 1) for i in range(inner - 1)])  3.15 us
    ppermute x1, waiting for transfers between devices, forward(): return lax.ppermute(value, 'inner', [(i, i + 1) for i in range(inner - 1)])  2.97 us
    ppermute x1, starting transfers between devices, backward(): return lax.ppermute(value, 'inner', [(i + 1, i) for i in range(inner - 1)])  1.92 us
    pallas_call x1, Pallas kernels, pack(): pl.pallas_call(pack_kernel, out_shape=in_vmem((2 * length, width), jnp.bf...  1.18 us
  transfers between devices with their start and end apart: 6, of which 4 were waited for; matrix products, arithmetic and copies ran while one was open for 0% of the time, Pallas kernels for 10%

profile of v3, /device:TPU:1, one launch (start us, length us, event | category | flops | bytes accessed | tf_op | source)
XLA Modules:
  0.0 44.1 jit_solution(14807395844416574954)
XLA Ops:
  0.6 0.0 copy-start
  0.6 0.0 copy-start.1
  0.7 1.2 %pack.1.refs_3_ = bf16[512,256]{1,0:T(8,128)(2,1)S(1)} custom-call(s32[2,2]{1,0:T(2,128)} %bitcast.17, s32[2,2]{1,0:T(2,128)} %bitcast.18, bf16[256,256]{1,0:T(8,128)(2,1)} %bitcast.15, bf16[256,256]{1,0:T(8,128)(2,1)} %bitcast.16), custom_call_target="tpu_custom_call" | custom-call | flops 8000000000 | bytes 1048576 | tf_op jit(solution)/shard_map/pack/pallas_call | solution.py:72
  1.8 5.7 %collective-permute-start.1 = (bf16[512,256]{1,0:T(8,128)(2,1)S(1)}, bf16[512,256]{1,0:T(8,128)(2,1)S(1)}, u32[]{:S(2)}, u32[]{:S(2)}) collective-permute-start(bf16[512,256]{1,0:T(8,128)(2,1)S(1)} %pack.1.refs_3_), channel_id=1, source_target_pairs={{0,256},{256,0},{1,257},{257,1},{2,258},{258,2},{3,259},{259,3},{4... | collective-permute-start | bytes 786440 | tf_op jit(solution)/shard_map/ppermute | solution.py:261
  7.5 3.1 %collective-permute-start = (bf16[512,256]{1,0:T(8,128)(2,1)S(1)}, bf16[512,256]{1,0:T(8,128)(2,1)S(1)}, u32[]{:S(2)}, u32[]{:S(2)}) collective-permute-start(bf16[512,256]{1,0:T(8,128)(2,1)S(1)} %pack.1.refs_3_), channel_id=1, source_target_pairs={{0,16},{16,32},{32,48},{48,64},{64,80},{80,96},{96,112},{112,128},... | collective-permute-start | bytes 786440 | tf_op jit(solution)/shard_map/ppermute | solution.py:255
  10.7 2.3 %collective-permute-start.2 = (bf16[512,256]{1,0:T(8,128)(2,1)S(1)}, bf16[512,256]{1,0:T(8,128)(2,1)S(1)}, u32[]{:S(2)}, u32[]{:S(2)}) collective-permute-start(bf16[512,256]{1,0:T(8,128)(2,1)S(1)} %pack.1.refs_3_), channel_id=1, source_target_pairs={{0,272},{16,288},{32,304},{48,320},{64,336},{80,352},{96,368},{112... | collective-permute-start | bytes 786440 | tf_op jit(solution)/shard_map/ppermute | solution.py:269
  13.6 0.0 collective-permute-done.1.refs_5_.refs_3_
  13.6 3.0 %collective-permute-done.refs_4_ = bf16[512,256]{1,0:T(8,128)(2,1)S(1)} collective-permute-done((bf16[512,256]{1,0:T(8,128)(2,1)S(1)}, bf16[512,256]{1,0:T(8,128)(2,1)S(1)}, u32[]{:S(2)}, u32[]{:S(2)}) %collective-permute-start) | collective-permute-done | bytes 262176 | tf_op jit(solution)/shard_map/ppermute | solution.py:255
  16.6 0.0 copy-done
  16.6 0.0 copy-done.1
  16.6 4.5 %attend_local.1 = (bf16[128,4096]{1,0:T(8,128)(2,1)}, bf16[512,256]{1,0:T(8,128)(2,1)S(1)}, f32[512,256]{1,0:T(8,128)S(1)}, bf16[512,128]{1,0:T(8,128)(2,1)S(1)}) custom-call(s32[1,1]{1,0:T(1,128)S(6)} %copy.12.refs_0_, bf16[128,4096]{1,0:T(8,128)(2,1)S(1)} %bitcast.11, bf16[128,4096]{1,0:T(8,128)(2,1)S(1)} %bitcast.13, bf16[512,256]{1,0:T(8,128)(2,1)S(1)} %pack.1.refs_3_, ...), custom_call_target="tpu_custom_call" | custom-call | flops 1342177280 | bytes 4194304 | tf_op jit(solution)/shard_map/attend_local/pallas_call | solution.py:223
  21.1 0.5 %collective-permute-done.2.refs_4_ = bf16[512,256]{1,0:T(8,128)(2,1)S(1)} collective-permute-done((bf16[512,256]{1,0:T(8,128)(2,1)S(1)}, bf16[512,256]{1,0:T(8,128)(2,1)S(1)}, u32[]{:S(2)}, u32[]{:S(2)}) %collective-permute-start.2) | collective-permute-done | bytes 262176 | tf_op jit(solution)/shard_map/ppermute | solution.py:269
  21.6 4.4 %attend_remote.1 = (bf16[128,4096]{1,0:T(8,128)(2,1)}, bf16[512,256]{1,0:T(8,128)(2,1)S(1)}, bf16[512,256]{1,0:T(8,128)(2,1)S(1)}) custom-call(bf16[512,128]{1,0:T(8,128)(2,1)S(1)} %get-tuple-element.10.refs_0_, bf16[128,4096]{1,0:T(8,128)(2,1)S(1)} %bitcast.12, bf16[128,4096]{1,0:T(8,128)(2,1)S(1)} %bitcast.14, ...), custom_call_target="tpu_custom_call", output_to_operand_aliasing={{0}: (5, {})} | custom-call | flops 1342177280 | bytes 4194304 | tf_op jit(solution)/shard_map/attend_remote/pallas_call | solution.py:223
  26.0 3.3 %collective-permute-start.4 = (bf16[512,256]{1,0:T(8,128)(2,1)S(1)}, bf16[512,256]{1,0:T(8,128)(2,1)S(1)}, u32[]{:S(2)}, u32[]{:S(2)}) collective-permute-start(bf16[512,256]{1,0:T(8,128)(2,1)S(1)} %get-tuple-element.15), channel_id=1, source_target_pairs={{0,256},{256,0},{1,257},{257,1},{2,258},{258,2},{3,259},{259,3},{4... | collective-permute-start | bytes 786440 | tf_op jit(solution)/shard_map/ppermute | solution.py:261
  29.3 6.0 %collective-permute-start.5 = (bf16[512,256]{1,0:T(8,128)(2,1)S(1)}, bf16[512,256]{1,0:T(8,128)(2,1)S(1)}, u32[]{:S(2)}, u32[]{:S(2)}) collective-permute-start(bf16[512,256]{1,0:T(8,128)(2,1)S(1)} %get-tuple-element.16), channel_id=1, source_target_pairs={{16,256},{32,272},{48,288},{64,304},{80,320},{96,336},{112,352},{1... | collective-permute-start | bytes 786440 | tf_op jit(solution)/shard_map/ppermute | solution.py:269
  35.4 1.9 %collective-permute-start.3 = (bf16[512,256]{1,0:T(8,128)(2,1)S(1)}, bf16[512,256]{1,0:T(8,128)(2,1)S(1)}, u32[]{:S(2)}, u32[]{:S(2)}) collective-permute-start(bf16[512,256]{1,0:T(8,128)(2,1)S(1)} %get-tuple-element.14), channel_id=1, source_target_pairs={{16,0},{32,16},{48,32},{64,48},{80,64},{96,80},{112,96},{128,112},... | collective-permute-start | bytes 786440 | tf_op jit(solution)/shard_map/ppermute | solution.py:258
  37.3 0.0 collective-permute-done.4
  37.3 5.8 %collective-permute-done.5 = bf16[512,256]{1,0:T(8,128)(2,1)S(1)} collective-permute-done((bf16[512,256]{1,0:T(8,128)(2,1)S(1)}, bf16[512,256]{1,0:T(8,128)(2,1)S(1)}, u32[]{:S(2)}, u32[]{:S(2)}) %collective-permute-start.5) | collective-permute-done | bytes 262176 | tf_op jit(solution)/shard_map/ppermute | solution.py:269
  43.1 0.2 collective-permute-done.3
  43.3 0.1 add_convert_fusion
  43.4 0.7 %slice_bitcast_fusion = (bf16[1,1,256,256]{3,2,1,0:T(8,128)(2,1)}, bf16[1,1,256,256]{3,2,1,0:T(8,128)(2,1)}) fusion(bf16[512,256]{1,0:T(8,128)(2,1)S(1)} %add_convert_fusion), kind=kLoop, calls=%fused_computation.1 | loop fusion | bytes 524288 | tf_op jit(solution)/shard_map/broadcast_in_dim | solution.py:288
Async XLA Ops:
  0.6 16.0 %copy-start = (bf16[1,1,128,4096]{3,2,1,0:T(8,128)(2,1)S(1)}, bf16[1,1,128,4096]{3,2,1,0:T(8,128)(2,1)}, u32[]{:S(2)}) copy-start(bf16[1,1,128,4096]{3,2,1,0:T(8,128)(2,1)} %param.7) | copy-start | bytes 3145732
  0.6 15.9 %copy-start.1 = (bf16[1,1,128,4096]{3,2,1,0:T(8,128)(2,1)S(1)}, bf16[1,1,128,4096]{3,2,1,0:T(8,128)(2,1)}, u32[]{:S(2)}) copy-start(bf16[1,1,128,4096]{3,2,1,0:T(8,128)(2,1)} %param.8) | copy-start | bytes 3145732
  1.8 11.8 %collective-permute-start.1 = (bf16[512,256]{1,0:T(8,128)(2,1)S(1)}, bf16[512,256]{1,0:T(8,128)(2,1)S(1)}, u32[]{:S(2)}, u32[]{:S(2)}) collective-permute-start(bf16[512,256]{1,0:T(8,128)(2,1)S(1)} %pack.1.refs_3_), channel_id=1, source_target_pairs={{0,256},{256,0},{1,257},{257,1},{2,258},{258,2},{3,259},{259,3},{4... | collective-permute-start | bytes 786440 | tf_op jit(solution)/shard_map/ppermute | solution.py:261
  7.5 9.1 %collective-permute-start = (bf16[512,256]{1,0:T(8,128)(2,1)S(1)}, bf16[512,256]{1,0:T(8,128)(2,1)S(1)}, u32[]{:S(2)}, u32[]{:S(2)}) collective-permute-start(bf16[512,256]{1,0:T(8,128)(2,1)S(1)} %pack.1.refs_3_), channel_id=1, source_target_pairs={{0,16},{16,32},{32,48},{48,64},{64,80},{80,96},{96,112},{112,128},... | collective-permute-start | bytes 786440 | tf_op jit(solution)/shard_map/ppermute | solution.py:255
  10.7 10.9 %collective-permute-start.2 = (bf16[512,256]{1,0:T(8,128)(2,1)S(1)}, bf16[512,256]{1,0:T(8,128)(2,1)S(1)}, u32[]{:S(2)}, u32[]{:S(2)}) collective-permute-start(bf16[512,256]{1,0:T(8,128)(2,1)S(1)} %pack.1.refs_3_), channel_id=1, source_target_pairs={{0,272},{16,288},{32,304},{48,320},{64,336},{80,352},{96,368},{112... | collective-permute-start | bytes 786440 | tf_op jit(solution)/shard_map/ppermute | solution.py:269
  26.0 11.3 %collective-permute-start.4 = (bf16[512,256]{1,0:T(8,128)(2,1)S(1)}, bf16[512,256]{1,0:T(8,128)(2,1)S(1)}, u32[]{:S(2)}, u32[]{:S(2)}) collective-permute-start(bf16[512,256]{1,0:T(8,128)(2,1)S(1)} %get-tuple-element.15), channel_id=1, source_target_pairs={{0,256},{256,0},{1,257},{257,1},{2,258},{258,2},{3,259},{259,3},{4... | collective-permute-start | bytes 786440 | tf_op jit(solution)/shard_map/ppermute | solution.py:261
  29.3 13.8 %collective-permute-start.5 = (bf16[512,256]{1,0:T(8,128)(2,1)S(1)}, bf16[512,256]{1,0:T(8,128)(2,1)S(1)}, u32[]{:S(2)}, u32[]{:S(2)}) collective-permute-start(bf16[512,256]{1,0:T(8,128)(2,1)S(1)} %get-tuple-element.16), channel_id=1, source_target_pairs={{16,256},{32,272},{48,288},{64,304},{80,320},{96,336},{112,352},{1... | collective-permute-start | bytes 786440 | tf_op jit(solution)/shard_map/ppermute | solution.py:269
  35.4 7.9 %collective-permute-start.3 = (bf16[512,256]{1,0:T(8,128)(2,1)S(1)}, bf16[512,256]{1,0:T(8,128)(2,1)S(1)}, u32[]{:S(2)}, u32[]{:S(2)}) collective-permute-start(bf16[512,256]{1,0:T(8,128)(2,1)S(1)} %get-tuple-element.14), channel_id=1, source_target_pairs={{16,0},{32,16},{48,32},{64,48},{80,64},{96,80},{112,96},{128,112},... | collective-permute-start | bytes 786440 | tf_op jit(solution)/shard_map/ppermute | solution.py:258

commit v4 on v3

v4 whole, which is shorter than its diff:
```python
import functools

import jax
import jax.numpy as jnp
from jax import lax
from jax.experimental import pallas as pl
from jax.experimental.pallas import tpu as pltpu
from jax.sharding import PartitionSpec as P

QUERY_HEADS = 32
KEY_VALUE_HEADS = 4
HEAD_SIZE = 128
ROWS_PER_SCALE = 128
GROUP = QUERY_HEADS // KEY_VALUE_HEADS
FACTOR = HEAD_SIZE**-0.5
LOG2_E = 1.4426950408889634
NEG_FILL = -1e30
PAIR = 8
PACK_FLOPS = 8 * 10**9
PACK_VMEM = 48


def nt(a, b):
    return lax.dot_general(a, b, (((1,), (1,)), ((), ())), preferred_element_type=jnp.float32)


def nn(a, b):
    return lax.dot_general(a, b, (((1,), (0,)), ((), ())), preferred_element_type=jnp.float32)


def in_vmem(shape, dtype):
    return pltpu.VMEM(shape, dtype)


def pinned(value, space):
    return pltpu.with_memory_space_constraint(value, space)


def pack_kernel(
    key_exps_hbm, value_exps_hbm, key_hbm, value_hbm, out_ref, key_ref, value_ref, key_exps, value_exps, sem
):
    length = key_ref.shape[0]
    loads = [
        pltpu.make_async_copy(key_hbm, key_ref, sem.at[0]),
        pltpu.make_async_copy(value_hbm, value_ref, sem.at[1]),
        pltpu.make_async_copy(key_exps_hbm, key_exps, sem.at[2]),
        pltpu.make_async_copy(value_exps_hbm, value_exps, sem.at[3]),
    ]
    for load in loads:
        load.start()
    for load in loads[2:]:
        load.wait()
    for load, source, exps, base in (
        (loads[0], key_ref, key_exps, 0),
        (loads[1], value_ref, value_exps, length),
    ):
        load.wait()
        for run in range(length // ROWS_PER_SCALE):
            part = slice(run * ROWS_PER_SCALE, (run + 1) * ROWS_PER_SCALE)
            to = slice(base + part.start, base + part.stop)
            for head in range(source.shape[1] // HEAD_SIZE):
                at = slice(head * HEAD_SIZE, (head + 1) * HEAD_SIZE)
                exponent = jnp.full((8, HEAD_SIZE), exps[run, head], jnp.int32).astype(jnp.float32)
                scale = jnp.exp2(exponent)[:1].astype(jnp.bfloat16)
                out_ref[to, at] = source[part, at] * scale


def pack(key_mant, value_mant, key_exps, value_exps):
    length, width = key_mant.shape
    vmem = pl.BlockSpec(memory_space=pltpu.VMEM)
    hbm = pl.BlockSpec(memory_space=pltpu.HBM)
    return pl.pallas_call(
        pack_kernel,
        out_shape=in_vmem((2 * length, width), jnp.bfloat16),
        in_specs=[hbm] * 4,
        out_specs=vmem,
        scratch_shapes=[
            pltpu.VMEM((length, width), jnp.bfloat16),
            pltpu.VMEM((length, width), jnp.bfloat16),
            pltpu.SMEM(key_exps.shape, jnp.int32),
            pltpu.SMEM(value_exps.shape, jnp.int32),
            pltpu.SemaphoreType.DMA((4,)),
        ],
        cost_estimate=pl.CostEstimate(flops=PACK_FLOPS, bytes_accessed=1024 * 1024, transcendentals=0),
        compiler_params=pltpu.CompilerParams(vmem_limit_bytes=PACK_VMEM * 1024 * 1024),
        name="pack",
    )(*(pinned(x, pltpu.HBM) for x in (key_exps, value_exps, key_mant, value_mant)))


def fetch(reach_hbm, reach_ref, bias_ref, q_ref, sem):
    group = lax.axis_index("head")
    bound = pltpu.make_async_copy(reach_hbm, reach_ref, sem.at[0])
    bound.start()
    tokens = q_ref.shape[0]
    length = bias_ref.shape[0] // 2
    rows = lax.broadcasted_iota(jnp.int32, bias_ref.shape, 0)
    cols = lax.broadcasted_iota(jnp.int32, bias_ref.shape, 1)
    last = jnp.where(rows < length, length, cols + (length + group * tokens))
    bound.wait()
    lowest = jnp.where(lax.axis_index("inner") == 0, length, length - reach_ref[...])
    visible = jnp.logical_and(rows >= lowest, rows <= last)
    bias_ref[...] = jnp.where(visible, 0.0, NEG_FILL).astype(jnp.bfloat16)


def columns(group, head):
    return pl.ds(pl.multiple_of((group * 2 * GROUP + head) * HEAD_SIZE, HEAD_SIZE), HEAD_SIZE)


def stacked(ref, group, kv):
    heads = range(kv * GROUP, (kv + 1) * GROUP)
    return jnp.concatenate([ref[:, columns(group, h)] for h in heads], axis=0)


def identity(tokens):
    down = lax.broadcasted_iota(jnp.int32, (tokens, tokens), 0)
    along = lax.broadcasted_iota(jnp.int32, (tokens, tokens), 1)
    one = jnp.where(down == along, 1.0, 0.0).astype(jnp.bfloat16)
    return jnp.concatenate([one] * GROUP, axis=0)


def project(keys, values, bias, queries, grads, ident):
    keys = jnp.concatenate([keys, bias], axis=1)
    scores = nt(keys, jnp.concatenate([queries, ident], axis=1))
    return scores, nt(values, grads)


def weigh(scores, peak):
    return jnp.exp2((scores - peak) * (FACTOR * LOG2_E))


def down(value):
    return jnp.sum(value, axis=0, keepdims=True)


def query_grad(dq_ref, keys, dscore, kv):
    tokens = dq_ref.shape[0]
    dq = (nn(keys.T, dscore) * FACTOR).astype(jnp.bfloat16).T
    for i in range(GROUP):
        head = kv * GROUP + i
        dq_ref[:, head * HEAD_SIZE : (head + 1) * HEAD_SIZE] = dq[i * tokens : (i + 1) * tokens]


def sender(group, dq_ref, dq_hbm, sem):
    wide = GROUP * HEAD_SIZE

    def send(kv):
        at = slice(kv * wide, (kv + 1) * wide)
        to = pl.ds(pl.multiple_of((group * 2 + kv) * wide, wide), wide)
        return pltpu.make_async_copy(dq_ref.at[:, at], dq_hbm.at[:, to], sem.at[kv])

    return send


def local_kernel(
    reach_hbm, q_ref, g_ref, own_ref, prev_ref, other_ref,
    dq_hbm, next_ref, term_ref, bias_ref, w_ref, d_ref, stat_ref,
    dq_ref, sem, load_sem, reach_ref,
):
    fetch(reach_hbm, reach_ref, bias_ref, q_ref, load_sem)
    tokens = q_ref.shape[0]
    length = own_ref.shape[0] // 2
    heads = own_ref.shape[1] // HEAD_SIZE
    group = lax.axis_index("head")
    bias = bias_ref[...]
    ident = identity(tokens)
    send = sender(group, dq_ref, dq_hbm, sem)

    def both(top, kv):
        at = slice(kv * HEAD_SIZE, (kv + 1) * HEAD_SIZE)
        part = slice(top, top + length)
        return jnp.concatenate([prev_ref[part, at], own_ref[part, at]], axis=0)

    def start(kv):
        return project(
            both(0, kv), both(length, kv), bias,
            stacked(q_ref, group, kv), stacked(g_ref, group, kv), ident,
        )

    def start_other(kv):
        at = slice(kv * HEAD_SIZE, (kv + 1) * HEAD_SIZE)
        return project(
            other_ref[:length, at], other_ref[length:, at], bias[length:],
            stacked(q_ref, 1 - group, kv), stacked(g_ref, 1 - group, kv), ident,
        )

    raw = start(0)
    for kv in range(heads):
        scores, dprob = raw
        raw = start(kv + 1) if kv + 1 < heads else start_other(0)
        weights = weigh(scores, jnp.max(scores, axis=0, keepdims=True))
        inverse = 1.0 / down(weights)
        row_dot = down(weights * dprob) * inverse
        probs = weights * inverse
        dscore = (probs * (dprob - row_dot)).astype(jnp.bfloat16)
        probs = probs.astype(jnp.bfloat16)
        query_grad(dq_ref, both(0, kv), dscore, kv)
        send(kv).start()
        dk = nn(dscore, stacked(q_ref, group, kv)) * FACTOR
        dv = nn(probs, stacked(g_ref, group, kv))
        at = slice(kv * HEAD_SIZE, (kv + 1) * HEAD_SIZE)
        next_ref[:length, at] = dk[:length].astype(next_ref.dtype)
        next_ref[length:, at] = dv[:length].astype(next_ref.dtype)
        term_ref[:length, at] = dk[length:]
        term_ref[length:, at] = dv[length:]
    for kv in range(heads):
        scores, dprob = raw
        raw = start_other(kv + 1) if kv + 1 < heads else None
        peak = jnp.max(scores, axis=0, keepdims=True)
        weights = weigh(scores, peak)
        at = slice(kv * GROUP * HEAD_SIZE, (kv + 1) * GROUP * HEAD_SIZE)
        w_ref[:, at] = weights
        d_ref[:, at] = dprob
        stat_ref[0:1, at] = peak
        stat_ref[1:2, at] = down(weights)
        stat_ref[2:3, at] = down(weights * dprob)
    for kv in range(heads):
        send(kv).wait()


def remote_kernel(bias_ref, q_ref, g_ref, prev_ref, w_ref, d_ref, stat_ref, next_ref, term_ref, z_ref):
    tokens = q_ref.shape[0]
    length = prev_ref.shape[0] // 2
    heads = prev_ref.shape[1] // HEAD_SIZE
    group = 1 - lax.axis_index("head")
    bias = bias_ref[:length]
    ident = identity(tokens)

    def start(kv):
        at = slice(kv * HEAD_SIZE, (kv + 1) * HEAD_SIZE)
        return project(
            prev_ref[:length, at], prev_ref[length:, at], bias,
            stacked(q_ref, group, kv), stacked(g_ref, group, kv), ident,
        )

    raw = start(0)
    for kv in range(heads):
        scores, dprob = raw
        raw = start(kv + 1) if kv + 1 < heads else None
        wide = slice(kv * GROUP * HEAD_SIZE, (kv + 1) * GROUP * HEAD_SIZE)
        before = stat_ref[0:1, wide]
        peak = jnp.maximum(jnp.max(scores, axis=0, keepdims=True), before)
        shrink = weigh(before, peak)
        weights = weigh(scores, peak)
        inverse = 1.0 / (down(weights) + shrink * stat_ref[1:2, wide])
        row_dot = (down(weights * dprob) + shrink * stat_ref[2:3, wide]) * inverse
        queries, grads = stacked(q_ref, group, kv), stacked(g_ref, group, kv)
        at = slice(kv * HEAD_SIZE, (kv + 1) * HEAD_SIZE)
        for ref, top, part, scale, grad in (
            (next_ref, 0, weights, inverse, dprob),
            (term_ref, length, w_ref[:, wide], shrink * inverse, d_ref[:, wide]),
        ):
            probs = part * scale
            dscore = (probs * (grad - row_dot)).astype(jnp.bfloat16)
            z_ref[top : top + length, wide] = dscore
            ref[:length, at] = (nn(dscore, queries) * FACTOR).astype(ref.dtype)
            ref[length:, at] = nn(probs.astype(jnp.bfloat16), grads).astype(ref.dtype)


def last_kernel(z_ref, own_ref, prev_ref, _, dq_hbm, dq_ref, sem):
    length = own_ref.shape[0] // 2
    heads = own_ref.shape[1] // HEAD_SIZE
    send = sender(1 - lax.axis_index("head"), dq_ref, dq_hbm, sem)
    for kv in range(heads):
        at = slice(kv * HEAD_SIZE, (kv + 1) * HEAD_SIZE)
        wide = slice(kv * GROUP * HEAD_SIZE, (kv + 1) * GROUP * HEAD_SIZE)
        keys = jnp.concatenate([prev_ref[:length, at], own_ref[:length, at]], axis=0)
        query_grad(dq_ref, keys, z_ref[:, wide], kv)
        send(kv).start()
    for kv in range(heads):
        send(kv).wait()


def call(kernel, operands, spaces, outs, scratch, flops, name, aliases=None):
    specs = {
        pltpu.VMEM: pl.BlockSpec(memory_space=pltpu.VMEM),
        pl.ANY: pl.BlockSpec(memory_space=pl.ANY),
    }
    return pl.pallas_call(
        kernel,
        out_shape=tuple(
            in_vmem(shape, dtype) if space is pltpu.VMEM else jax.ShapeDtypeStruct(shape, dtype)
            for space, shape, dtype in outs
        ),
        in_specs=[specs[space] for space in spaces],
        out_specs=tuple(specs[space] for space, _, _ in outs),
        scratch_shapes=scratch,
        input_output_aliases=aliases or {},
        cost_estimate=pl.CostEstimate(flops=flops, bytes_accessed=4 * 1024 * 1024, transcendentals=0),
        compiler_params=pltpu.CompilerParams(vmem_limit_bytes=32 * 1024 * 1024),
        name=name,
    )(*(pinned(x, space) if space is pltpu.VMEM else x for x, space in zip(operands, spaces)))


def on_device(query, dout, key_mant, value_mantissas, key_exps, value_exponents, reach):
    inner = lax.axis_size("inner")
    length = key_mant.shape[2]
    own = pack(key_mant[0, 0], value_mantissas[0, 0], key_exps[0, 0], value_exponents[0, 0])

    def forward(value):
        return lax.ppermute(value, "inner", [(i, i + 1) for i in range(inner - 1)])

    def backward(value):
        return lax.ppermute(value, "inner", [(i + 1, i) for i in range(inner - 1)])

    def swap(value):
        return lax.ppermute(value, "head", [(0, 1), (1, 0)])

    def across(value, step):
        pairs = [
            (head * inner + at, (1 - head) * inner + at + step)
            for head in range(2)
            for at in range(max(0, -step), min(inner, inner - step))
        ]
        return lax.ppermute(value, ("head", "inner"), pairs)

    prev = forward(own)
    other_own = swap(own)
    other_prev = across(own, 1)
    loads = (reach, pinned(query[0, 0], pltpu.VMEM), pinned(dout[0, 0], pltpu.VMEM))
    reach, query, dout = loads
    rows, half = own.shape
    tokens, width = query.shape
    lanes = width // 2
    fast, anywhere, bf16, f32 = pltpu.VMEM, pl.ANY, jnp.bfloat16, jnp.float32
    flops = 12 * lanes * rows * HEAD_SIZE
    stage = [pltpu.VMEM((tokens, lanes), bf16), pltpu.SemaphoreType.DMA((2,))]
    dq, next_here, term_here, bias, weights, dprob, stats = call(
        local_kernel,
        (reach, query, dout, own, prev, other_own),
        (anywhere, fast, fast, fast, fast, fast),
        (
            (anywhere, (tokens, width), bf16),
            (fast, (rows, half), bf16),
            (fast, (rows, half), f32),
            (fast, (rows, tokens), bf16),
            (fast, (length, lanes), f32),
            (fast, (length, lanes), f32),
            (fast, (8, lanes), f32),
        ),
        stage + [pltpu.SemaphoreType.DMA((1,)), pltpu.VMEM((1, 1), jnp.int32)],
        flops,
        "local",
    )
    returned = backward(next_here)
    next_there, term_there, dscore = call(
        remote_kernel,
        (bias, query, dout, other_prev, weights, dprob, stats),
        (fast,) * 7,
        ((fast, (rows, half), bf16), (fast, (rows, half), bf16), (fast, (rows, lanes), bf16)),
        [],
        flops,
        "remote",
    )
    swapped = swap(term_there)
    crossed = across(next_there, -1)
    (dq,) = call(
        last_kernel,
        (dscore, other_own, other_prev, dq),
        (fast, fast, fast, anywhere),
        ((anywhere, (tokens, width), bf16),),
        stage,
        flops,
        "last",
        {3: 0},
    )
    total = term_here
    for part in (returned, swapped, crossed):
        total = total + part.astype(jnp.float32)
    total = total.astype(jnp.bfloat16)
    return dq[None, None], total[None, None, :length], total[None, None, length:]


def solution(mesh):
    placed = (
        P("outer", "inner", "head", None),
        P("outer", "inner", "head", None),
        P("outer", "inner", None, "head"),
        P("outer", "inner", None, "head"),
        P("outer", "inner", None, "head"),
        P("outer", "inner", None, "head"),
        P("outer", "inner"),
    )
    return jax.shard_map(
        on_device,
        mesh=mesh,
        in_specs=placed,
        out_specs=(
            P("outer", "inner", "head", None),
            P("outer", "inner", None, "head"),
            P("outer", "inner", None, "head"),
        ),
        check_vma=False,
    )
```

time: 44.5 us -> 43.8 us (0.984)
  waiting for transfers between devices: 9.44 us -> 7.74 us
  Pallas kernels: 10.1 us -> 10.7 us
    ppermute x2, waiting for transfers between devices: 6.26 us -> 4.22 us  [across(): return lax.ppermute(value, ('head', 'inner'), pairs)]
    ppermute x2, starting transfers between devices: 8.33 us -> 9.4 us  [across(): return lax.ppermute(value, ('head', 'inner'), pairs)]
    ppermute x2, starting transfers between devices: 8.98 us -> 8.38 us  [swap(): return lax.ppermute(value, 'head', [(0, 1), (1, 0)])]
    pallas_call x2 -> x3, Pallas kernels: 8.91 us -> 9.5 us  [call(): pl.pallas_call(kernel, out_shape=tuple((in_vmem(shape, dtype) if space is...]
  transfers between devices with their start and end apart: 6 -> 6, of which waited for: 4 -> 3; matrix products, arithmetic and copies ran while one was open for 0% -> 0% of each run, Pallas kernels for 10% -> 16%
where the time goes in v4:
time: 43.8 us; the launch traced here: 43.5 us
  starting transfers between devices  22.8 us (52%)
  Pallas kernels  10.7 us (24%)
  waiting for transfers between devices  7.74 us (18%)
  between operations  1.4 us (3%)
  local copies, waits for them, and re-layouts  0.72 us (2%)
    pallas_call x3, Pallas kernels, call(): pl.pallas_call(kernel, out_shape=tuple((in_vmem(shape, dtype) if space is...  9.5 us
    ppermute x2, starting transfers between devices, across(): return lax.ppermute(value, ('head', 'inner'), pairs)  9.4 us
    ppermute x2, starting transfers between devices, swap(): return lax.ppermute(value, 'head', [(0, 1), (1, 0)])  8.38 us
    ppermute x2, waiting for transfers between devices, across(): return lax.ppermute(value, ('head', 'inner'), pairs)  4.22 us
    ppermute x1, starting transfers between devices, forward(): return lax.ppermute(value, 'inner', [(i, i + 1) for i in range(inner - 1)])  3.15 us
    ppermute x1, waiting for transfers between devices, forward(): return lax.ppermute(value, 'inner', [(i, i + 1) for i in range(inner - 1)])  2.97 us
    ppermute x1, starting transfers between devices, backward(): return lax.ppermute(value, 'inner', [(i + 1, i) for i in range(inner - 1)])  1.92 us
    pallas_call x1, Pallas kernels, pack(): pl.pallas_call(pack_kernel, out_shape=in_vmem((2 * length, width), jnp.bf...  1.18 us
  transfers between devices with their start and end apart: 6, of which 3 were waited for; matrix products, arithmetic and copies ran while one was open for 0% of the time, Pallas kernels for 16%

profile of v4, /device:TPU:1, one launch (start us, length us, event | category | flops | bytes accessed | tf_op | source)
XLA Modules:
  0.0 43.5 jit_solution(11203958845926463118)
XLA Ops:
  0.6 0.0 copy-start
  0.6 0.0 copy-start.1
  0.7 1.2 %pack.1.own_ref = bf16[512,256]{1,0:T(8,128)(2,1)S(1)} custom-call(s32[2,2]{1,0:T(2,128)} %bitcast.17, s32[2,2]{1,0:T(2,128)} %bitcast.18, bf16[256,256]{1,0:T(8,128)(2,1)} %bitcast.15, bf16[256,256]{1,0:T(8,128)(2,1)} %bitcast.16), custom_call_target="tpu_custom_call" | custom-call | flops 8000000000 | bytes 1048576 | tf_op jit(solution)/shard_map/pack/pallas_call | solution.py:72
  1.8 5.7 %collective-permute-start.1 = (bf16[512,256]{1,0:T(8,128)(2,1)S(1)}, bf16[512,256]{1,0:T(8,128)(2,1)S(1)}, u32[]{:S(2)}, u32[]{:S(2)}) collective-permute-start(bf16[512,256]{1,0:T(8,128)(2,1)S(1)} %pack.1.own_ref), channel_id=1, source_target_pairs={{0,256},{256,0},{1,257},{257,1},{2,258},{258,2},{3,259},{259,3},{4... | collective-permute-start | bytes 786440 | tf_op jit(solution)/shard_map/ppermute | solution.py:306
  7.5 3.1 %collective-permute-start = (bf16[512,256]{1,0:T(8,128)(2,1)S(1)}, bf16[512,256]{1,0:T(8,128)(2,1)S(1)}, u32[]{:S(2)}, u32[]{:S(2)}) collective-permute-start(bf16[512,256]{1,0:T(8,128)(2,1)S(1)} %pack.1.own_ref), channel_id=1, source_target_pairs={{0,16},{16,32},{32,48},{48,64},{64,80},{80,96},{96,112},{112,128},... | collective-permute-start | bytes 786440 | tf_op jit(solution)/shard_map/ppermute | solution.py:300
  10.7 2.3 %collective-permute-start.2 = (bf16[512,256]{1,0:T(8,128)(2,1)S(1)}, bf16[512,256]{1,0:T(8,128)(2,1)S(1)}, u32[]{:S(2)}, u32[]{:S(2)}) collective-permute-start(bf16[512,256]{1,0:T(8,128)(2,1)S(1)} %pack.1.own_ref), channel_id=1, source_target_pairs={{0,272},{16,288},{32,304},{48,320},{64,336},{80,352},{96,368},{112... | collective-permute-start | bytes 786440 | tf_op jit(solution)/shard_map/ppermute | solution.py:314
  13.6 0.0 collective-permute-done.1.other_ref.own_ref
  13.6 3.0 %collective-permute-done.prev_ref = bf16[512,256]{1,0:T(8,128)(2,1)S(1)} collective-permute-done((bf16[512,256]{1,0:T(8,128)(2,1)S(1)}, bf16[512,256]{1,0:T(8,128)(2,1)S(1)}, u32[]{:S(2)}, u32[]{:S(2)}) %collective-permute-start) | collective-permute-done | bytes 262176 | tf_op jit(solution)/shard_map/ppermute | solution.py:300
  16.6 0.0 copy-done
  16.6 0.0 copy-done.1
  16.6 5.5 %local.1 = (bf16[128,4096]{1,0:T(8,128)(2,1)}, bf16[512,256]{1,0:T(8,128)(2,1)S(1)}, f32[512,256]{1,0:T(8,128)S(1)}, bf16[512,128]{1,0:T(8,128)(2,1)S(1)}, f32[2...) custom-call(s32[1,1]{1,0:T(1,128)S(6)} %copy.12.reach_hbm, bf16[128,4096]{1,0:T(8,128)(2,1)S(1)} %bitcast.11, ...), custom_call_target="tpu_custom_call" | custom-call | flops 1610612736 | bytes 4194304 | tf_op jit(solution)/shard_map/local/pallas_call | solution.py:278
  22.1 0.0 collective-permute-done.2.prev_ref
  22.1 2.7 %remote.1 = (bf16[512,256]{1,0:T(8,128)(2,1)S(1)}, bf16[512,256]{1,0:T(8,128)(2,1)S(1)}, bf16[512,2048]{1,0:T(8,128)(2,1)S(1)}) custom-call(bf16[512,128]{1,0:T(8,128)(2,1)S(1)} %get-tuple-element.13.bias_ref, bf16[128,4096]{1,0:T(8,128)(2,1)S(1)} %bitcast.12, bf16[128,4096]{1,0:T(8,128)(2,1)S(1)} %bitcast.14, ...), custom_call_target="tpu_custom_call" | custom-call | flops 1610612736 | bytes 4194304 | tf_op jit(solution)/shard_map/remote/pallas_call | solution.py:278
  24.8 2.7 %collective-permute-start.4 = (bf16[512,256]{1,0:T(8,128)(2,1)S(1)}, bf16[512,256]{1,0:T(8,128)(2,1)S(1)}, u32[]{:S(2)}, u32[]{:S(2)}) collective-permute-start(bf16[512,256]{1,0:T(8,128)(2,1)S(1)} %get-tuple-element.21), channel_id=1, source_target_pairs={{0,256},{256,0},{1,257},{257,1},{2,258},{258,2},{3,259},{259,3},{4... | collective-permute-start | bytes 786440 | tf_op jit(solution)/shard_map/ppermute | solution.py:306
  27.6 7.1 %collective-permute-start.5 = (bf16[512,256]{1,0:T(8,128)(2,1)S(1)}, bf16[512,256]{1,0:T(8,128)(2,1)S(1)}, u32[]{:S(2)}, u32[]{:S(2)}) collective-permute-start(bf16[512,256]{1,0:T(8,128)(2,1)S(1)} %get-tuple-element.22), channel_id=1, source_target_pairs={{16,256},{32,272},{48,288},{64,304},{80,320},{96,336},{112,352},{1... | collective-permute-start | bytes 786440 | tf_op jit(solution)/shard_map/ppermute | solution.py:314
  34.7 1.9 %collective-permute-start.3 = (bf16[512,256]{1,0:T(8,128)(2,1)S(1)}, bf16[512,256]{1,0:T(8,128)(2,1)S(1)}, u32[]{:S(2)}, u32[]{:S(2)}) collective-permute-start(bf16[512,256]{1,0:T(8,128)(2,1)S(1)} %get-tuple-element.20), channel_id=1, source_target_pairs={{16,0},{32,16},{48,32},{64,48},{80,64},{96,80},{112,96},{128,112},... | collective-permute-start | bytes 786440 | tf_op jit(solution)/shard_map/ppermute | solution.py:303
  36.6 1.3 %last.1 = bf16[128,4096]{1,0:T(8,128)(2,1)} custom-call(bf16[512,2048]{1,0:T(8,128)(2,1)S(1)} %get-tuple-element.17.z_ref, bf16[512,256]{1,0:T(8,128)(2,1)S(1)} %collective-permute-done.1.other_ref.own_ref, bf16[512,256]{1,0:T(8,128)(2,1)S(1)} %collective-permute-done.2.prev_ref, bf16[128,4096]{1,0:T(8,128)(2,1)} %get-tuple-element.18._), custom_call_target="tpu_custom_call", output_to_operand_aliasing={{}: (3, {})} | custom-call | flops 1610612736 | bytes 4194304 | tf_op jit(solution)/shard_map/last/pallas_call | solution.py:278
  37.9 0.0 collective-permute-done.4
  37.9 4.2 %collective-permute-done.5 = bf16[512,256]{1,0:T(8,128)(2,1)S(1)} collective-permute-done((bf16[512,256]{1,0:T(8,128)(2,1)S(1)}, bf16[512,256]{1,0:T(8,128)(2,1)S(1)}, u32[]{:S(2)}, u32[]{:S(2)}) %collective-permute-start.5) | collective-permute-done | bytes 262176 | tf_op jit(solution)/shard_map/ppermute | solution.py:314
  42.1 0.5 %collective-permute-done.3 = bf16[512,256]{1,0:T(8,128)(2,1)S(1)} collective-permute-done((bf16[512,256]{1,0:T(8,128)(2,1)S(1)}, bf16[512,256]{1,0:T(8,128)(2,1)S(1)}, u32[]{:S(2)}, u32[]{:S(2)}) %collective-permute-start.3) | collective-permute-done | bytes 262176 | tf_op jit(solution)/shard_map/ppermute | solution.py:303
  42.7 0.1 add_convert_fusion
  42.8 0.7 %slice_bitcast_fusion = (bf16[1,1,256,256]{3,2,1,0:T(8,128)(2,1)}, bf16[1,1,256,256]{3,2,1,0:T(8,128)(2,1)}) fusion(bf16[512,256]{1,0:T(8,128)(2,1)S(1)} %add_convert_fusion), kind=kLoop, calls=%fused_computation.1 | loop fusion | bytes 524288 | tf_op jit(solution)/shard_map/broadcast_in_dim | solution.py:370
Async XLA Ops:
  0.6 16.0 %copy-start = (bf16[1,1,128,4096]{3,2,1,0:T(8,128)(2,1)S(1)}, bf16[1,1,128,4096]{3,2,1,0:T(8,128)(2,1)}, u32[]{:S(2)}) copy-start(bf16[1,1,128,4096]{3,2,1,0:T(8,128)(2,1)} %param.7) | copy-start | bytes 3145732
  0.6 15.9 %copy-start.1 = (bf16[1,1,128,4096]{3,2,1,0:T(8,128)(2,1)S(1)}, bf16[1,1,128,4096]{3,2,1,0:T(8,128)(2,1)}, u32[]{:S(2)}) copy-start(bf16[1,1,128,4096]{3,2,1,0:T(8,128)(2,1)} %param.8) | copy-start | bytes 3145732
  1.8 11.8 %collective-permute-start.1 = (bf16[512,256]{1,0:T(8,128)(2,1)S(1)}, bf16[512,256]{1,0:T(8,128)(2,1)S(1)}, u32[]{:S(2)}, u32[]{:S(2)}) collective-permute-start(bf16[512,256]{1,0:T(8,128)(2,1)S(1)} %pack.1.own_ref), channel_id=1, source_target_pairs={{0,256},{256,0},{1,257},{257,1},{2,258},{258,2},{3,259},{259,3},{4... | collective-permute-start | bytes 786440 | tf_op jit(solution)/shard_map/ppermute | solution.py:306
  7.5 9.1 %collective-permute-start = (bf16[512,256]{1,0:T(8,128)(2,1)S(1)}, bf16[512,256]{1,0:T(8,128)(2,1)S(1)}, u32[]{:S(2)}, u32[]{:S(2)}) collective-permute-start(bf16[512,256]{1,0:T(8,128)(2,1)S(1)} %pack.1.own_ref), channel_id=1, source_target_pairs={{0,16},{16,32},{32,48},{48,64},{64,80},{80,96},{96,112},{112,128},... | collective-permute-start | bytes 786440 | tf_op jit(solution)/shard_map/ppermute | solution.py:300
  10.7 11.5 %collective-permute-start.2 = (bf16[512,256]{1,0:T(8,128)(2,1)S(1)}, bf16[512,256]{1,0:T(8,128)(2,1)S(1)}, u32[]{:S(2)}, u32[]{:S(2)}) collective-permute-start(bf16[512,256]{1,0:T(8,128)(2,1)S(1)} %pack.1.own_ref), channel_id=1, source_target_pairs={{0,272},{16,288},{32,304},{48,320},{64,336},{80,352},{96,368},{112... | collective-permute-start | bytes 786440 | tf_op jit(solution)/shard_map/ppermute | solution.py:314
  24.8 13.1 %collective-permute-start.4 = (bf16[512,256]{1,0:T(8,128)(2,1)S(1)}, bf16[512,256]{1,0:T(8,128)(2,1)S(1)}, u32[]{:S(2)}, u32[]{:S(2)}) collective-permute-start(bf16[512,256]{1,0:T(8,128)(2,1)S(1)} %get-tuple-element.21), channel_id=1, source_target_pairs={{0,256},{256,0},{1,257},{257,1},{2,258},{258,2},{3,259},{259,3},{4... | collective-permute-start | bytes 786440 | tf_op jit(solution)/shard_map/ppermute | solution.py:306
  27.6 14.5 %collective-permute-start.5 = (bf16[512,256]{1,0:T(8,128)(2,1)S(1)}, bf16[512,256]{1,0:T(8,128)(2,1)S(1)}, u32[]{:S(2)}, u32[]{:S(2)}) collective-permute-start(bf16[512,256]{1,0:T(8,128)(2,1)S(1)} %get-tuple-element.22), channel_id=1, source_target_pairs={{16,256},{32,272},{48,288},{64,304},{80,320},{96,336},{112,352},{1... | collective-permute-start | bytes 786440 | tf_op jit(solution)/shard_map/ppermute | solution.py:314
  34.7 8.0 %collective-permute-start.3 = (bf16[512,256]{1,0:T(8,128)(2,1)S(1)}, bf16[512,256]{1,0:T(8,128)(2,1)S(1)}, u32[]{:S(2)}, u32[]{:S(2)}) collective-permute-start(bf16[512,256]{1,0:T(8,128)(2,1)S(1)} %get-tuple-element.20), channel_id=1, source_target_pairs={{16,0},{32,16},{48,32},{64,48},{80,64},{96,80},{112,96},{128,112},... | collective-permute-start | bytes 786440 | tf_op jit(solution)/shard_map/ppermute | solution.py:303

commit v5 on v4

--- a/solution.py
+++ b/solution.py
@@ -152,8 +152,8 @@
 
 
 def local_kernel(
-    reach_hbm, q_ref, g_ref, own_ref, prev_ref, other_ref,
-    dq_hbm, next_ref, term_ref, bias_ref, w_ref, d_ref, stat_ref,
+    reach_hbm, q_ref, g_ref, own_ref, prev_ref,
+    dq_hbm, next_ref, term_ref, bias_ref,
     dq_ref, sem, load_sem, reach_ref,
 ):
     fetch(reach_hbm, reach_ref, bias_ref, q_ref, load_sem)
@@ -176,17 +176,10 @@
             stacked(q_ref, group, kv), stacked(g_ref, group, kv), ident,
         )
 
-    def start_other(kv):
-        at = slice(kv * HEAD_SIZE, (kv + 1) * HEAD_SIZE)
-        return project(
-            other_ref[:length, at], other_ref[length:, at], bias[length:],
-            stacked(q_ref, 1 - group, kv), stacked(g_ref, 1 - group, kv), ident,
-        )
-
     raw = start(0)
     for kv in range(heads):
         scores, dprob = raw
-        raw = start(kv + 1) if kv + 1 < heads else start_other(0)
+        raw = start(kv + 1) if kv + 1 < heads else None
         weights = weigh(scores, jnp.max(scores, axis=0, keepdims=True))
         inverse = 1.0 / down(weights)
         row_dot = down(weights * dprob) * inverse
@@ -203,8 +196,28 @@
         term_ref[:length, at] = dk[length:]
         term_ref[length:, at] = dv[length:]
     for kv in range(heads):
+        send(kv).wait()
+
+
+def partial_kernel(bias_ref, q_ref, g_ref, other_ref, w_ref, d_ref, stat_ref):
+    tokens = q_ref.shape[0]
+    length = other_ref.shape[0] // 2
+    heads = other_ref.shape[1] // HEAD_SIZE
+    group = 1 - lax.axis_index("head")
+    bias = bias_ref[length:]
+    ident = identity(tokens)
+
+    def start(kv):
+        at = slice(kv * HEAD_SIZE, (kv + 1) * HEAD_SIZE)
+        return project(
+            other_ref[:length, at], other_ref[length:, at], bias,
+            stacked(q_ref, group, kv), stacked(g_ref, group, kv), ident,
+        )
+
+    raw = start(0)
+    for kv in range(heads):
         scores, dprob = raw
-        raw = start_other(kv + 1) if kv + 1 < heads else None
+        raw = start(kv + 1) if kv + 1 < heads else None
         peak = jnp.max(scores, axis=0, keepdims=True)
         weights = weigh(scores, peak)
         at = slice(kv * GROUP * HEAD_SIZE, (kv + 1) * GROUP * HEAD_SIZE)
@@ -213,8 +226,6 @@
         stat_ref[0:1, at] = peak
         stat_ref[1:2, at] = down(weights)
         stat_ref[2:3, at] = down(weights * dprob)
-    for kv in range(heads):
-        send(kv).wait()
 
 
 def remote_kernel(bias_ref, q_ref, g_ref, prev_ref, w_ref, d_ref, stat_ref, next_ref, term_ref, z_ref):
@@ -256,7 +267,7 @@
             ref[length:, at] = nn(probs.astype(jnp.bfloat16), grads).astype(ref.dtype)
 
 
-def last_kernel(z_ref, own_ref, prev_ref, _, dq_hbm, dq_ref, sem):
+def last_kernel(z_ref, own_ref, prev_ref, term_ref, back_ref, _, dq_hbm, sum_ref, dq_ref, sem):
     length = own_ref.shape[0] // 2
     heads = own_ref.shape[1] // HEAD_SIZE
     send = sender(1 - lax.axis_index("head"), dq_ref, dq_hbm, sem)
@@ -266,6 +277,7 @@
         keys = jnp.concatenate([prev_ref[:length, at], own_ref[:length, at]], axis=0)
         query_grad(dq_ref, keys, z_ref[:, wide], kv)
         send(kv).start()
+    sum_ref[...] = term_ref[...] + back_ref[...].astype(jnp.float32)
     for kv in range(heads):
         send(kv).wait()
 
@@ -324,24 +336,30 @@
     fast, anywhere, bf16, f32 = pltpu.VMEM, pl.ANY, jnp.bfloat16, jnp.float32
     flops = 12 * lanes * rows * HEAD_SIZE
     stage = [pltpu.VMEM((tokens, lanes), bf16), pltpu.SemaphoreType.DMA((2,))]
-    dq, next_here, term_here, bias, weights, dprob, stats = call(
+    dq, next_here, term_here, bias = call(
         local_kernel,
-        (reach, query, dout, own, prev, other_own),
-        (anywhere, fast, fast, fast, fast, fast),
+        (reach, query, dout, own, prev),
+        (anywhere, fast, fast, fast, fast),
         (
             (anywhere, (tokens, width), bf16),
             (fast, (rows, half), bf16),
             (fast, (rows, half), f32),
             (fast, (rows, tokens), bf16),
-            (fast, (length, lanes), f32),
-            (fast, (length, lanes), f32),
-            (fast, (8, lanes), f32),
         ),
         stage + [pltpu.SemaphoreType.DMA((1,)), pltpu.VMEM((1, 1), jnp.int32)],
         flops,
         "local",
     )
     returned = backward(next_here)
+    weights, dprob, stats = call(
+        partial_kernel,
+        (bias, query, dout, other_own),
+        (fast,) * 4,
+        ((fast, (length, lanes), f32), (fast, (length, lanes), f32), (fast, (8, lanes), f32)),
+        [],
+        flops // 4,
+        "partial",
+    )
     next_there, term_there, dscore = call(
         remote_kernel,
         (bias, query, dout, other_prev, weights, dprob, stats),
@@ -353,18 +371,17 @@
     )
     swapped = swap(term_there)
     crossed = across(next_there, -1)
-    (dq,) = call(
+    dq, total = call(
         last_kernel,
-        (dscore, other_own, other_prev, dq),
-        (fast, fast, fast, anywhere),
-        ((anywhere, (tokens, width), bf16),),
+        (dscore, other_own, other_prev, term_here, returned, dq),
+        (fast, fast, fast, fast, fast, anywhere),
+        ((anywhere, (tokens, width), bf16), (fast, (rows, half), f32)),
         stage,
         flops,
         "last",
-        {3: 0},
-    )
-    total = term_here
-    for part in (returned, swapped, crossed):
+        {5: 0},
+    )
+    for part in (crossed, swapped):
         total = total + part.astype(jnp.float32)
     total = total.astype(jnp.bfloat16)
     return dq[None, None], total[None, None, :length], total[None, None, length:]

time: 43.8 us -> 43 us (0.982); the launches traced: 43.5 us -> 42.2 us
  starting transfers between devices: 22.8 us -> 19.7 us
  waiting for transfers between devices: 7.74 us -> 9.62 us
    ppermute x2, waiting for transfers between devices: 4.22 us -> 9.61 us  [across(): return lax.ppermute(value, ('head', 'inner'), pairs)]
    ppermute x2, starting transfers between devices: 9.4 us -> 5.35 us  [across(): return lax.ppermute(value, ('head', 'inner'), pairs)]
    ppermute x1, waiting for transfers between devices: 2.97 us -> 0.01 us  [forward(): return lax.ppermute(value, 'inner', [(i, i + 1) for i in range(inner - 1)])]
    ppermute x1, starting transfers between devices: 3.15 us -> 4.59 us  [forward(): return lax.ppermute(value, 'inner', [(i, i + 1) for i in range(inner - 1)])]
    ppermute x2, starting transfers between devices: 8.38 us -> 7.18 us  [swap(): return lax.ppermute(value, 'head', [(0, 1), (1, 0)])]
    ppermute x1, starting transfers between devices: 1.92 us -> 2.6 us  [backward(): return lax.ppermute(value, 'inner', [(i + 1, i) for i in range(inner - 1)])]
    ppermute x1, waiting for transfers between devices: 0.55 us -> 0.01 us  [backward(): return lax.ppermute(value, 'inner', [(i + 1, i) for i in range(inner - 1)])]
    pallas_call x3 -> x4, Pallas kernels: 9.5 us -> 9.43 us  [call(): pl.pallas_call(kernel, out_shape=tuple((in_vmem(shape, dtype) if space is...]
  transfers between devices with their start and end apart: 6 -> 6, of which waited for: 3 -> 2; matrix products, arithmetic and copies ran while one was open for 0% -> 0% of each run, Pallas kernels for 16% -> 22%
where the time goes in v5:
time: 43 us; the launch traced here: 42.2 us
  starting transfers between devices  19.7 us (46%)
  Pallas kernels  10.6 us (25%)
  waiting for transfers between devices  9.62 us (22%)
  between operations  1.42 us (3%)
  local copies, waits for them, and re-layouts  0.72 us (2%)
    ppermute x2, waiting for transfers between devices, across(): return lax.ppermute(value, ('head', 'inner'), pairs)  9.61 us
    pallas_call x4, Pallas kernels, call(): pl.pallas_call(kernel, out_shape=tuple((in_vmem(shape, dtype) if space is...  9.43 us
    ppermute x2, starting transfers between devices, swap(): return lax.ppermute(value, 'head', [(0, 1), (1, 0)])  7.18 us
    ppermute x2, starting transfers between devices, across(): return lax.ppermute(value, ('head', 'inner'), pairs)  5.35 us
    ppermute x1, starting transfers between devices, forward(): return lax.ppermute(value, 'inner', [(i, i + 1) for i in range(inner - 1)])  4.59 us
    ppermute x1, starting transfers between devices, backward(): return lax.ppermute(value, 'inner', [(i + 1, i) for i in range(inner - 1)])  2.6 us
    pallas_call x1, Pallas kernels, pack(): pl.pallas_call(pack_kernel, out_shape=in_vmem((2 * length, width), jnp.bf...  1.18 us
  transfers between devices with their start and end apart: 6, of which 2 were waited for; matrix products, arithmetic and copies ran while one was open for 0% of the time, Pallas kernels for 22%

profile of v5, /device:TPU:1, one launch (start us, length us, event | category | flops | bytes accessed | tf_op | source)
XLA Modules:
  0.0 42.2 jit_solution(18022780842762310091)
XLA Ops:
  0.6 0.0 copy-start
  0.6 0.0 copy-start.1
  0.7 1.2 %pack.1.own_ref = bf16[512,256]{1,0:T(8,128)(2,1)S(1)} custom-call(s32[2,2]{1,0:T(2,128)} %bitcast.19, s32[2,2]{1,0:T(2,128)} %bitcast.20, bf16[256,256]{1,0:T(8,128)(2,1)} %bitcast.17, bf16[256,256]{1,0:T(8,128)(2,1)} %bitcast.18), custom_call_target="tpu_custom_call" | custom-call | flops 8000000000 | bytes 1048576 | tf_op jit(solution)/shard_map/pack/pallas_call | solution.py:72
  1.8 4.6 %collective-permute-start = (bf16[512,256]{1,0:T(8,128)(2,1)S(1)}, bf16[512,256]{1,0:T(8,128)(2,1)S(1)}, u32[]{:S(2)}, u32[]{:S(2)}) collective-permute-start(bf16[512,256]{1,0:T(8,128)(2,1)S(1)} %pack.1.own_ref), channel_id=1, source_target_pairs={{0,16},{16,32},{32,48},{48,64},{64,80},{80,96},{96,112},{112,128},... | collective-permute-start | bytes 786440 | tf_op jit(solution)/shard_map/ppermute | solution.py:312
  6.4 4.5 %collective-permute-start.2 = (bf16[512,256]{1,0:T(8,128)(2,1)S(1)}, bf16[512,256]{1,0:T(8,128)(2,1)S(1)}, u32[]{:S(2)}, u32[]{:S(2)}) collective-permute-start(bf16[512,256]{1,0:T(8,128)(2,1)S(1)} %pack.1.own_ref), channel_id=1, source_target_pairs={{0,256},{256,0},{1,257},{257,1},{2,258},{258,2},{3,259},{259,3},{4... | collective-permute-start | bytes 786440 | tf_op jit(solution)/shard_map/ppermute | solution.py:318
  11.0 2.0 %collective-permute-start.1 = (bf16[512,256]{1,0:T(8,128)(2,1)S(1)}, bf16[512,256]{1,0:T(8,128)(2,1)S(1)}, u32[]{:S(2)}, u32[]{:S(2)}) collective-permute-start(bf16[512,256]{1,0:T(8,128)(2,1)S(1)} %pack.1.own_ref), channel_id=1, source_target_pairs={{0,272},{16,288},{32,304},{48,320},{64,336},{80,352},{96,368},{112... | collective-permute-start | bytes 786440 | tf_op jit(solution)/shard_map/ppermute | solution.py:326
  13.6 0.0 collective-permute-done.prev_ref
  13.6 0.0 copy-done
  13.6 0.0 copy-done.1
  13.6 4.5 %local.1 = (bf16[128,4096]{1,0:T(8,128)(2,1)}, bf16[512,256]{1,0:T(8,128)(2,1)S(1)}, f32[512,256]{1,0:T(8,128)S(1)}, bf16[512,128]{1,0:T(8,128)(2,1)S(1)}) custom-call(s32[1,1]{1,0:T(1,128)S(6)} %copy.12.reach_hbm, bf16[128,4096]{1,0:T(8,128)(2,1)S(1)} %bitcast.11, bf16[128,4096]{1,0:T(8,128)(2,1)S(1)} %bitcast.14, bf16[512,256]{1,0:T(8,128)(2,1)S(1)} %pack.1.own_ref, ...), custom_call_target="tpu_custom_call" | custom-call | flops 1610612736 | bytes 4194304 | tf_op jit(solution)/shard_map/local/pallas_call | solution.py:290
  18.1 2.6 %collective-permute-start.3 = (bf16[512,256]{1,0:T(8,128)(2,1)S(1)}, bf16[512,256]{1,0:T(8,128)(2,1)S(1)}, u32[]{:S(2)}, u32[]{:S(2)}) collective-permute-start(bf16[512,256]{1,0:T(8,128)(2,1)S(1)} %get-tuple-element.21), channel_id=1, source_target_pairs={{16,0},{32,16},{48,32},{64,48},{80,64},{96,80},{112,96},{128,112},... | collective-permute-start | bytes 786440 | tf_op jit(solution)/shard_map/ppermute | solution.py:315
  20.8 0.0 collective-permute-done.2.other_ref.own_ref
  20.8 1.0 %partial.1 = (f32[256,2048]{1,0:T(8,128)S(1)}, f32[256,2048]{1,0:T(8,128)S(1)}, f32[8,2048]{1,0:T(8,128)S(1)}) custom-call(bf16[512,128]{1,0:T(8,128)(2,1)S(1)} %get-tuple-element.15.bias_ref, bf16[128,4096]{1,0:T(8,128)(2,1)S(1)} %bitcast.12, bf16[128,4096]{1,0:T(8,128)(2,1)S(1)} %bitcast.15, bf16[512,256]{1,0:T(8,128)(2,1)S(1)} %collective-permute-done.2.other_ref.own_ref), custom_call_target="tpu_custom_call" | custom-call | flops 402653184 | bytes 4194304 | tf_op jit(solution)/shard_map/partial/pallas_call | solution.py:290
  21.7 0.7 %collective-permute-done.1.prev_ref = bf16[512,256]{1,0:T(8,128)(2,1)S(1)} collective-permute-done((bf16[512,256]{1,0:T(8,128)(2,1)S(1)}, bf16[512,256]{1,0:T(8,128)(2,1)S(1)}, u32[]{:S(2)}, u32[]{:S(2)}) %collective-permute-start.1) | collective-permute-done | bytes 262176 | tf_op jit(solution)/shard_map/ppermute | solution.py:326
  22.4 2.7 %remote.1 = (bf16[512,256]{1,0:T(8,128)(2,1)S(1)}, bf16[512,256]{1,0:T(8,128)(2,1)S(1)}, bf16[512,2048]{1,0:T(8,128)(2,1)S(1)}) custom-call(bf16[512,128]{1,0:T(8,128)(2,1)S(1)} %get-tuple-element.15.bias_ref, bf16[128,4096]{1,0:T(8,128)(2,1)S(1)} %bitcast.13, bf16[128,4096]{1,0:T(8,128)(2,1)S(1)} %bitcast.16, ...), custom_call_target="tpu_custom_call" | custom-call | flops 1610612736 | bytes 4194304 | tf_op jit(solution)/shard_map/remote/pallas_call | solution.py:290
  25.1 3.4 %collective-permute-start.4 = (bf16[512,256]{1,0:T(8,128)(2,1)S(1)}, bf16[512,256]{1,0:T(8,128)(2,1)S(1)}, u32[]{:S(2)}, u32[]{:S(2)}) collective-permute-start(bf16[512,256]{1,0:T(8,128)(2,1)S(1)} %get-tuple-element.25), channel_id=1, source_target_pairs={{16,256},{32,272},{48,288},{64,304},{80,320},{96,336},{112,352},{1... | collective-permute-start | bytes 786440 | tf_op jit(solution)/shard_map/ppermute | solution.py:326
  28.5 2.6 %collective-permute-start.5 = (bf16[512,256]{1,0:T(8,128)(2,1)S(1)}, bf16[512,256]{1,0:T(8,128)(2,1)S(1)}, u32[]{:S(2)}, u32[]{:S(2)}) collective-permute-start(bf16[512,256]{1,0:T(8,128)(2,1)S(1)} %get-tuple-element.26), channel_id=1, source_target_pairs={{0,256},{256,0},{1,257},{257,1},{2,258},{258,2},{3,259},{259,3},{4... | collective-permute-start | bytes 786440 | tf_op jit(solution)/shard_map/ppermute | solution.py:318
  31.1 0.0 collective-permute-done.3.back_ref
  31.1 1.3 %last.1 = (bf16[128,4096]{1,0:T(8,128)(2,1)}, f32[512,256]{1,0:T(8,128)S(1)}) custom-call(bf16[512,2048]{1,0:T(8,128)(2,1)S(1)} %get-tuple-element.19.z_ref, bf16[512,256]{1,0:T(8,128)(2,1)S(1)} %collective-permute-done.2.other_ref.own_ref, bf16[512,256]{1,0:T(8,128)(2,1)S(1)} %collective-permute-done.1.prev_ref, ...), custom_call_target="tpu_custom_call", output_to_operand_aliasing={{0}: (5, {})} | custom-call | flops 1610612736 | bytes 4194304 | tf_op jit(solution)/shard_map/last/pallas_call | solution.py:290
  32.4 8.9 %collective-permute-done.4 = bf16[512,256]{1,0:T(8,128)(2,1)S(1)} collective-permute-done((bf16[512,256]{1,0:T(8,128)(2,1)S(1)}, bf16[512,256]{1,0:T(8,128)(2,1)S(1)}, u32[]{:S(2)}, u32[]{:S(2)}) %collective-permute-start.4) | collective-permute-done | bytes 262176 | tf_op jit(solution)/shard_map/ppermute | solution.py:326
  41.4 0.0 collective-permute-done.5
  41.4 0.1 add_convert_fusion
  41.5 0.7 %slice_bitcast_fusion = (bf16[1,1,256,256]{3,2,1,0:T(8,128)(2,1)}, bf16[1,1,256,256]{3,2,1,0:T(8,128)(2,1)}) fusion(bf16[512,256]{1,0:T(8,128)(2,1)S(1)} %add_convert_fusion), kind=kLoop, calls=%fused_computation.1 | loop fusion | bytes 524288 | tf_op jit(solution)/shard_map/broadcast_in_dim | solution.py:387
Async XLA Ops:
  0.6 13.0 %copy-start = (bf16[1,1,128,4096]{3,2,1,0:T(8,128)(2,1)S(1)}, bf16[1,1,128,4096]{3,2,1,0:T(8,128)(2,1)}, u32[]{:S(2)}) copy-start(bf16[1,1,128,4096]{3,2,1,0:T(8,128)(2,1)} %param.7) | copy-start | bytes 3145732
  0.6 13.0 %copy-start.1 = (bf16[1,1,128,4096]{3,2,1,0:T(8,128)(2,1)S(1)}, bf16[1,1,128,4096]{3,2,1,0:T(8,128)(2,1)}, u32[]{:S(2)}) copy-start(bf16[1,1,128,4096]{3,2,1,0:T(8,128)(2,1)} %param.8) | copy-start | bytes 3145732
  1.8 11.8 %collective-permute-start = (bf16[512,256]{1,0:T(8,128)(2,1)S(1)}, bf16[512,256]{1,0:T(8,128)(2,1)S(1)}, u32[]{:S(2)}, u32[]{:S(2)}) collective-permute-start(bf16[512,256]{1,0:T(8,128)(2,1)S(1)} %pack.1.own_ref), channel_id=1, source_target_pairs={{0,16},{16,32},{32,48},{48,64},{64,80},{80,96},{96,112},{112,128},... | collective-permute-start | bytes 786440 | tf_op jit(solution)/shard_map/ppermute | solution.py:312
  6.4 14.3 %collective-permute-start.2 = (bf16[512,256]{1,0:T(8,128)(2,1)S(1)}, bf16[512,256]{1,0:T(8,128)(2,1)S(1)}, u32[]{:S(2)}, u32[]{:S(2)}) collective-permute-start(bf16[512,256]{1,0:T(8,128)(2,1)S(1)} %pack.1.own_ref), channel_id=1, source_target_pairs={{0,256},{256,0},{1,257},{257,1},{2,258},{258,2},{3,259},{259,3},{4... | collective-permute-start | bytes 786440 | tf_op jit(solution)/shard_map/ppermute | solution.py:318
  11.0 11.4 %collective-permute-start.1 = (bf16[512,256]{1,0:T(8,128)(2,1)S(1)}, bf16[512,256]{1,0:T(8,128)(2,1)S(1)}, u32[]{:S(2)}, u32[]{:S(2)}) collective-permute-start(bf16[512,256]{1,0:T(8,128)(2,1)S(1)} %pack.1.own_ref), channel_id=1, source_target_pairs={{0,272},{16,288},{32,304},{48,320},{64,336},{80,352},{96,368},{112... | collective-permute-start | bytes 786440 | tf_op jit(solution)/shard_map/ppermute | solution.py:326
  18.1 13.0 %collective-permute-start.3 = (bf16[512,256]{1,0:T(8,128)(2,1)S(1)}, bf16[512,256]{1,0:T(8,128)(2,1)S(1)}, u32[]{:S(2)}, u32[]{:S(2)}) collective-permute-start(bf16[512,256]{1,0:T(8,128)(2,1)S(1)} %get-tuple-element.21), channel_id=1, source_target_pairs={{16,0},{32,16},{48,32},{64,48},{80,64},{96,80},{112,96},{128,112},... | collective-permute-start | bytes 786440 | tf_op jit(solution)/shard_map/ppermute | solution.py:315
  25.1 16.3 %collective-permute-start.4 = (bf16[512,256]{1,0:T(8,128)(2,1)S(1)}, bf16[512,256]{1,0:T(8,128)(2,1)S(1)}, u32[]{:S(2)}, u32[]{:S(2)}) collective-permute-start(bf16[512,256]{1,0:T(8,128)(2,1)S(1)} %get-tuple-element.25), channel_id=1, source_target_pairs={{16,256},{32,272},{48,288},{64,304},{80,320},{96,336},{112,352},{1... | collective-permute-start | bytes 786440 | tf_op jit(solution)/shard_map/ppermute | solution.py:326
  28.5 12.9 %collective-permute-start.5 = (bf16[512,256]{1,0:T(8,128)(2,1)S(1)}, bf16[512,256]{1,0:T(8,128)(2,1)S(1)}, u32[]{:S(2)}, u32[]{:S(2)}) collective-permute-start(bf16[512,256]{1,0:T(8,128)(2,1)S(1)} %get-tuple-element.26), channel_id=1, source_target_pairs={{0,256},{256,0},{1,257},{257,1},{2,258},{258,2},{3,259},{259,3},{4... | collective-permute-start | bytes 786440 | tf_op jit(solution)/shard_map/ppermute | solution.py:318

commit v6 on v5

--- a/solution.py
+++ b/solution.py
@@ -256,15 +256,19 @@
         row_dot = (down(weights * dprob) + shrink * stat_ref[2:3, wide]) * inverse
         queries, grads = stacked(q_ref, group, kv), stacked(g_ref, group, kv)
         at = slice(kv * HEAD_SIZE, (kv + 1) * HEAD_SIZE)
-        for ref, top, part, scale, grad in (
-            (next_ref, 0, weights, inverse, dprob),
-            (term_ref, length, w_ref[:, wide], shrink * inverse, d_ref[:, wide]),
+        parts = []
+        for part, scale, grad in (
+            (weights, inverse, dprob),
+            (w_ref[:, wide], shrink * inverse, d_ref[:, wide]),
         ):
             probs = part * scale
-            dscore = (probs * (grad - row_dot)).astype(jnp.bfloat16)
-            z_ref[top : top + length, wide] = dscore
-            ref[:length, at] = (nn(dscore, queries) * FACTOR).astype(ref.dtype)
-            ref[length:, at] = nn(probs.astype(jnp.bfloat16), grads).astype(ref.dtype)
+            parts.append((probs.astype(jnp.bfloat16), (probs * (grad - row_dot)).astype(jnp.bfloat16)))
+        probs, dscore = (jnp.concatenate(pair, axis=0) for pair in zip(*parts))
+        z_ref[:, wide] = dscore
+        dk, dv = nn(dscore, queries) * FACTOR, nn(probs, grads)
+        for ref, rows in ((next_ref, slice(0, length)), (term_ref, slice(length, 2 * length))):
+            ref[:length, at] = dk[rows].astype(ref.dtype)
+            ref[length:, at] = dv[rows].astype(ref.dtype)
 
 
 def last_kernel(z_ref, own_ref, prev_ref, term_ref, back_ref, _, dq_hbm, sum_ref, dq_ref, sem):
@@ -381,10 +385,11 @@
         "last",
         {5: 0},
     )
-    for part in (crossed, swapped):
-        total = total + part.astype(jnp.float32)
-    total = total.astype(jnp.bfloat16)
-    return dq[None, None], total[None, None, :length], total[None, None, length:]
+    outs = []
+    for rows in (slice(0, length), slice(length, 2 * length)):
+        part = total[rows] + crossed[rows].astype(f32) + swapped[rows].astype(f32)
+        outs.append(part.astype(bf16)[None, None])
+    return dq[None, None], *outs
 
 
 def solution(mesh):

time: 43 us -> 42.9 us (level)
  local copies, waits for them, and re-layouts: 0.72 us -> 0.01 us
  other arithmetic: 0.08 us -> 0.78 us
    broadcast_in_dim x0 -> x1, other arithmetic: none -> 0.78 us  [on_device(): outs.append(part.astype(bf16)[None, None])]
    broadcast_in_dim x1 -> x0, local copies, waits for them, and re-layouts: 0.72 us -> none  [on_device(): total[None, None, length:]]
where the time goes in v6:
time: 42.9 us; the launch traced here: 42.1 us
  starting transfers between devices  19.7 us (46%)
  Pallas kernels  10.6 us (25%)
  waiting for transfers between devices  9.62 us (22%)
  between operations  1.42 us (3%)
  other arithmetic  0.78 us (2%)
    ppermute x2, waiting for transfers between devices, across(): return lax.ppermute(value, ('head', 'inner'), pairs)  9.61 us
    pallas_call x4, Pallas kernels, call(): pl.pallas_call(kernel, out_shape=tuple((in_vmem(shape, dtype) if space is...  9.39 us
    ppermute x2, starting transfers between devices, swap(): return lax.ppermute(value, 'head', [(0, 1), (1, 0)])  7.18 us
    ppermute x2, starting transfers between devices, across(): return lax.ppermute(value, ('head', 'inner'), pairs)  5.34 us
    ppermute x1, starting transfers between devices, forward(): return lax.ppermute(value, 'inner', [(i, i + 1) for i in range(inner - 1)])  4.59 us
    ppermute x1, starting transfers between devices, backward(): return lax.ppermute(value, 'inner', [(i + 1, i) for i in range(inner - 1)])  2.6 us
    pallas_call x1, Pallas kernels, pack(): pl.pallas_call(pack_kernel, out_shape=in_vmem((2 * length, width), jnp.bf...  1.18 us
  transfers between devices with their start and end apart: 6, of which 2 were waited for; matrix products, arithmetic and copies ran while one was open for 0% of the time, Pallas kernels for 22%

profile of v6, /device:TPU:1, one launch (start us, length us, event | category | flops | bytes accessed | tf_op | source)
XLA Modules:
  0.0 42.1 jit_solution(3611930845206984748)
XLA Ops:
  0.6 0.0 copy-start
  0.6 0.0 copy-start.1
  0.7 1.2 %pack.1.own_ref = bf16[512,256]{1,0:T(8,128)(2,1)S(1)} custom-call(s32[2,2]{1,0:T(2,128)} %bitcast.19, s32[2,2]{1,0:T(2,128)} %bitcast.20, bf16[256,256]{1,0:T(8,128)(2,1)} %bitcast.17, bf16[256,256]{1,0:T(8,128)(2,1)} %bitcast.18), custom_call_target="tpu_custom_call" | custom-call | flops 8000000000 | bytes 1048576 | tf_op jit(solution)/shard_map/pack/pallas_call | solution.py:72
  1.8 4.6 %collective-permute-start = (bf16[512,256]{1,0:T(8,128)(2,1)S(1)}, bf16[512,256]{1,0:T(8,128)(2,1)S(1)}, u32[]{:S(2)}, u32[]{:S(2)}) collective-permute-start(bf16[512,256]{1,0:T(8,128)(2,1)S(1)} %pack.1.own_ref), channel_id=1, source_target_pairs={{0,16},{16,32},{32,48},{48,64},{64,80},{80,96},{96,112},{112,128},... | collective-permute-start | bytes 786440 | tf_op jit(solution)/shard_map/ppermute | solution.py:316
  6.4 4.5 %collective-permute-start.2 = (bf16[512,256]{1,0:T(8,128)(2,1)S(1)}, bf16[512,256]{1,0:T(8,128)(2,1)S(1)}, u32[]{:S(2)}, u32[]{:S(2)}) collective-permute-start(bf16[512,256]{1,0:T(8,128)(2,1)S(1)} %pack.1.own_ref), channel_id=1, source_target_pairs={{0,256},{256,0},{1,257},{257,1},{2,258},{258,2},{3,259},{259,3},{4... | collective-permute-start | bytes 786440 | tf_op jit(solution)/shard_map/ppermute | solution.py:322
  11.0 2.0 %collective-permute-start.1 = (bf16[512,256]{1,0:T(8,128)(2,1)S(1)}, bf16[512,256]{1,0:T(8,128)(2,1)S(1)}, u32[]{:S(2)}, u32[]{:S(2)}) collective-permute-start(bf16[512,256]{1,0:T(8,128)(2,1)S(1)} %pack.1.own_ref), channel_id=1, source_target_pairs={{0,272},{16,288},{32,304},{48,320},{64,336},{80,352},{96,368},{112... | collective-permute-start | bytes 786440 | tf_op jit(solution)/shard_map/ppermute | solution.py:330
  13.6 0.0 collective-permute-done.prev_ref
  13.6 0.0 copy-done
  13.6 0.0 copy-done.1
  13.6 4.5 %local.1 = (bf16[128,4096]{1,0:T(8,128)(2,1)}, bf16[512,256]{1,0:T(8,128)(2,1)S(1)}, f32[512,256]{1,0:T(8,128)S(1)}, bf16[512,128]{1,0:T(8,128)(2,1)S(1)}) custom-call(s32[1,1]{1,0:T(1,128)S(6)} %copy.12.reach_hbm, bf16[128,4096]{1,0:T(8,128)(2,1)S(1)} %bitcast.11, bf16[128,4096]{1,0:T(8,128)(2,1)S(1)} %bitcast.14, bf16[512,256]{1,0:T(8,128)(2,1)S(1)} %pack.1.own_ref, ...), custom_call_target="tpu_custom_call" | custom-call | flops 1610612736 | bytes 4194304 | tf_op jit(solution)/shard_map/local/pallas_call | solution.py:294
  18.1 2.6 %collective-permute-start.3 = (bf16[512,256]{1,0:T(8,128)(2,1)S(1)}, bf16[512,256]{1,0:T(8,128)(2,1)S(1)}, u32[]{:S(2)}, u32[]{:S(2)}) collective-permute-start(bf16[512,256]{1,0:T(8,128)(2,1)S(1)} %get-tuple-element.21), channel_id=1, source_target_pairs={{16,0},{32,16},{48,32},{64,48},{80,64},{96,80},{112,96},{128,112},... | collective-permute-start | bytes 786440 | tf_op jit(solution)/shard_map/ppermute | solution.py:319
  20.8 0.0 collective-permute-done.2.other_ref.own_ref
  20.8 1.0 %partial.1 = (f32[256,2048]{1,0:T(8,128)S(1)}, f32[256,2048]{1,0:T(8,128)S(1)}, f32[8,2048]{1,0:T(8,128)S(1)}) custom-call(bf16[512,128]{1,0:T(8,128)(2,1)S(1)} %get-tuple-element.15.bias_ref, bf16[128,4096]{1,0:T(8,128)(2,1)S(1)} %bitcast.12, bf16[128,4096]{1,0:T(8,128)(2,1)S(1)} %bitcast.15, bf16[512,256]{1,0:T(8,128)(2,1)S(1)} %collective-permute-done.2.other_ref.own_ref), custom_call_target="tpu_custom_call" | custom-call | flops 402653184 | bytes 4194304 | tf_op jit(solution)/shard_map/partial/pallas_call | solution.py:294
  21.7 0.7 %collective-permute-done.1.prev_ref = bf16[512,256]{1,0:T(8,128)(2,1)S(1)} collective-permute-done((bf16[512,256]{1,0:T(8,128)(2,1)S(1)}, bf16[512,256]{1,0:T(8,128)(2,1)S(1)}, u32[]{:S(2)}, u32[]{:S(2)}) %collective-permute-start.1) | collective-permute-done | bytes 262176 | tf_op jit(solution)/shard_map/ppermute | solution.py:330
  22.4 2.6 %remote.1 = (bf16[512,256]{1,0:T(8,128)(2,1)S(1)}, bf16[512,256]{1,0:T(8,128)(2,1)S(1)}, bf16[512,2048]{1,0:T(8,128)(2,1)S(1)}) custom-call(bf16[512,128]{1,0:T(8,128)(2,1)S(1)} %get-tuple-element.15.bias_ref, bf16[128,4096]{1,0:T(8,128)(2,1)S(1)} %bitcast.13, bf16[128,4096]{1,0:T(8,128)(2,1)S(1)} %bitcast.16, ...), custom_call_target="tpu_custom_call" | custom-call | flops 1610612736 | bytes 4194304 | tf_op jit(solution)/shard_map/remote/pallas_call | solution.py:294
  25.1 3.4 %collective-permute-start.4 = (bf16[512,256]{1,0:T(8,128)(2,1)S(1)}, bf16[512,256]{1,0:T(8,128)(2,1)S(1)}, u32[]{:S(2)}, u32[]{:S(2)}) collective-permute-start(bf16[512,256]{1,0:T(8,128)(2,1)S(1)} %get-tuple-element.25), channel_id=1, source_target_pairs={{16,256},{32,272},{48,288},{64,304},{80,320},{96,336},{112,352},{1... | collective-permute-start | bytes 786440 | tf_op jit(solution)/shard_map/ppermute | solution.py:330
  28.4 2.7 %collective-permute-start.5 = (bf16[512,256]{1,0:T(8,128)(2,1)S(1)}, bf16[512,256]{1,0:T(8,128)(2,1)S(1)}, u32[]{:S(2)}, u32[]{:S(2)}) collective-permute-start(bf16[512,256]{1,0:T(8,128)(2,1)S(1)} %get-tuple-element.26), channel_id=1, source_target_pairs={{0,256},{256,0},{1,257},{257,1},{2,258},{258,2},{3,259},{259,3},{4... | collective-permute-start | bytes 786440 | tf_op jit(solution)/shard_map/ppermute | solution.py:322
  31.1 0.0 collective-permute-done.3.back_ref
  31.1 1.3 %last.1 = (bf16[128,4096]{1,0:T(8,128)(2,1)}, f32[512,256]{1,0:T(8,128)S(1)}) custom-call(bf16[512,2048]{1,0:T(8,128)(2,1)S(1)} %get-tuple-element.19.z_ref, bf16[512,256]{1,0:T(8,128)(2,1)S(1)} %collective-permute-done.2.other_ref.own_ref, bf16[512,256]{1,0:T(8,128)(2,1)S(1)} %collective-permute-done.1.prev_ref, ...), custom_call_target="tpu_custom_call", output_to_operand_aliasing={{0}: (5, {})} | custom-call | flops 1610612736 | bytes 4194304 | tf_op jit(solution)/shard_map/last/pallas_call | solution.py:294
  32.4 8.9 %collective-permute-done.4 = bf16[512,256]{1,0:T(8,128)(2,1)S(1)} collective-permute-done((bf16[512,256]{1,0:T(8,128)(2,1)S(1)}, bf16[512,256]{1,0:T(8,128)(2,1)S(1)}, u32[]{:S(2)}, u32[]{:S(2)}) %collective-permute-start.4) | collective-permute-done | bytes 262176 | tf_op jit(solution)/shard_map/ppermute | solution.py:330
  41.3 0.0 collective-permute-done.5
  41.3 0.8 %fusion.1 = (bf16[1,1,256,256]{3,2,1,0:T(8,128)(2,1)}, bf16[1,1,256,256]{3,2,1,0:T(8,128)(2,1)}) fusion(f32[512,256]{1,0:T(8,128)S(1)} %get-tuple-element.24, bf16[512,256]{1,0:T(8,128)(2,1)S(1)} %collective-permute-done.5, bf16[512,256]{1,0:T(8,128)(2,1)S(1)} %collective-permute-done.4), kind=kLoop, calls=%fused_computation.3 | loop fusion | flops 655360 | bytes 1310720 | tf_op jit(solution)/shard_map/broadcast_in_dim | solution.py:391
Async XLA Ops:
  0.6 13.0 %copy-start = (bf16[1,1,128,4096]{3,2,1,0:T(8,128)(2,1)S(1)}, bf16[1,1,128,4096]{3,2,1,0:T(8,128)(2,1)}, u32[]{:S(2)}) copy-start(bf16[1,1,128,4096]{3,2,1,0:T(8,128)(2,1)} %param.7) | copy-start | bytes 3145732
  0.6 13.0 %copy-start.1 = (bf16[1,1,128,4096]{3,2,1,0:T(8,128)(2,1)S(1)}, bf16[1,1,128,4096]{3,2,1,0:T(8,128)(2,1)}, u32[]{:S(2)}) copy-start(bf16[1,1,128,4096]{3,2,1,0:T(8,128)(2,1)} %param.8) | copy-start | bytes 3145732
  1.8 11.8 %collective-permute-start = (bf16[512,256]{1,0:T(8,128)(2,1)S(1)}, bf16[512,256]{1,0:T(8,128)(2,1)S(1)}, u32[]{:S(2)}, u32[]{:S(2)}) collective-permute-start(bf16[512,256]{1,0:T(8,128)(2,1)S(1)} %pack.1.own_ref), channel_id=1, source_target_pairs={{0,16},{16,32},{32,48},{48,64},{64,80},{80,96},{96,112},{112,128},... | collective-permute-start | bytes 786440 | tf_op jit(solution)/shard_map/ppermute | solution.py:316
  6.4 14.3 %collective-permute-start.2 = (bf16[512,256]{1,0:T(8,128)(2,1)S(1)}, bf16[512,256]{1,0:T(8,128)(2,1)S(1)}, u32[]{:S(2)}, u32[]{:S(2)}) collective-permute-start(bf16[512,256]{1,0:T(8,128)(2,1)S(1)} %pack.1.own_ref), channel_id=1, source_target_pairs={{0,256},{256,0},{1,257},{257,1},{2,258},{258,2},{3,259},{259,3},{4... | collective-permute-start | bytes 786440 | tf_op jit(solution)/shard_map/ppermute | solution.py:322
  11.0 11.4 %collective-permute-start.1 = (bf16[512,256]{1,0:T(8,128)(2,1)S(1)}, bf16[512,256]{1,0:T(8,128)(2,1)S(1)}, u32[]{:S(2)}, u32[]{:S(2)}) collective-permute-start(bf16[512,256]{1,0:T(8,128)(2,1)S(1)} %pack.1.own_ref), channel_id=1, source_target_pairs={{0,272},{16,288},{32,304},{48,320},{64,336},{80,352},{96,368},{112... | collective-permute-start | bytes 786440 | tf_op jit(solution)/shard_map/ppermute | solution.py:330
  18.1 12.9 %collective-permute-start.3 = (bf16[512,256]{1,0:T(8,128)(2,1)S(1)}, bf16[512,256]{1,0:T(8,128)(2,1)S(1)}, u32[]{:S(2)}, u32[]{:S(2)}) collective-permute-start(bf16[512,256]{1,0:T(8,128)(2,1)S(1)} %get-tuple-element.21), channel_id=1, source_target_pairs={{16,0},{32,16},{48,32},{64,48},{80,64},{96,80},{112,96},{128,112},... | collective-permute-start | bytes 786440 | tf_op jit(solution)/shard_map/ppermute | solution.py:319
  25.1 16.3 %collective-permute-start.4 = (bf16[512,256]{1,0:T(8,128)(2,1)S(1)}, bf16[512,256]{1,0:T(8,128)(2,1)S(1)}, u32[]{:S(2)}, u32[]{:S(2)}) collective-permute-start(bf16[512,256]{1,0:T(8,128)(2,1)S(1)} %get-tuple-element.25), channel_id=1, source_target_pairs={{16,256},{32,272},{48,288},{64,304},{80,320},{96,336},{112,352},{1... | collective-permute-start | bytes 786440 | tf_op jit(solution)/shard_map/ppermute | solution.py:330
  28.4 12.9 %collective-permute-start.5 = (bf16[512,256]{1,0:T(8,128)(2,1)S(1)}, bf16[512,256]{1,0:T(8,128)(2,1)S(1)}, u32[]{:S(2)}, u32[]{:S(2)}) collective-permute-start(bf16[512,256]{1,0:T(8,128)(2,1)S(1)} %get-tuple-element.26), channel_id=1, source_target_pairs={{0,256},{256,0},{1,257},{257,1},{2,258},{258,2},{3,259},{259,3},{4... | collective-permute-start | bytes 786440 | tf_op jit(solution)/shard_map/ppermute | solution.py:322
